TPU v7x, 512 devices: a whole 4x4x16 slice. The times are simulated.
512 devices in a mesh: seq: 8 (over x, core), head: 64 (over y, z).
Axes of the slice: x: 4, y: 4, z: 16, core: 2. Of those that a mesh axis runs over, the one named last changes fastest.
Arguments:
- q_rot: bfloat16 [8192, 8192], P(('seq', 'head')), may hold values from -4 to 4
- k_rot: bfloat16 [8192, 1024], P(('seq', 'head')), may hold values from -7 to 7
- v_rot: bfloat16 [8192, 1024], P(('seq', 'head')), may hold values from -6 to 6
- q_exp: int32 [512, 256], P(('seq', 'head')), may hold values from 0 to 1
- k_exp: int32 [512, 32], P(('seq', 'head')), may hold values from 0 to 1
- v_exp: int32 [512, 32], P(('seq', 'head')), may hold values from -1 to 1
- span_order: int32 [16], replicated, may hold values from 0 to 15, each once
- ffn_row: int32 [8, 1024], P('seq'), may hold values from 0 to 1023, each once within a row
Outputs:
- routed: bfloat16 [8192, 8192], P(('seq', 'head'))
Inputs may be any that keep to these rules, and one draw needn't show every extreme that they name: `span_order`: each number of 0 to 15 once. Each row of ffn_row holds every number of 0 to 1023 once.
All inputs are finite; a program needn't handle non-finite values.
Results may differ from a plain program's by a relative error of at most 0.004.
Values may be sent and summed in bfloat16 or wider, within the bound.
No kernel may reach another device: no remote copies, remote signals or barrier semaphores. Data moves between devices by JAX's collectives and lax.ppermute only.
A program may use at most 64 MiB of HBM per device.

v0:
```python
import functools
import math

import jax
import jax.numpy as jnp
from jax import lax
from jax.experimental import pallas as pl
from jax.experimental.pallas import tpu as pltpu
from jax.sharding import Mesh, PartitionSpec as P

HD = 128
HBLK = 32
QBLK = 16
SPANS_GRP = 2
PARTS = 3
TAIL = 16
TILES = 2

NEG = -1e30
NT = (((1,), (1,)), ((), ()))
TN = (((0,), (0,)), ((), ()))
PLANE = ("y", "kv", "pair")
NEAR = ("core", "y")


def pack_kernel(q_ref, k_ref, v_ref, qe_ref, ke_ref, ve_ref, o_ref, *, n_y, n_kv, n_pair):
    tok = q_ref.shape[0]
    share = tok // n_y
    blocks = HD // HBLK
    spread = jnp.where(
        lax.broadcasted_iota(jnp.int32, (blocks, HD), 1) // HBLK == lax.broadcasted_iota(jnp.int32, (blocks, HD), 0),
        1.0,
        0.0,
    )

    def factors(ref):
        scale = jnp.exp2(ref[...].astype(jnp.float32))
        return sum(scale[:, b:b + 1] * spread[b:b + 1, :] for b in range(blocks))

    def head(ref, scale, n):
        return ref[:, n * HD:(n + 1) * HD].astype(jnp.float32) * scale[n:n + 1, :]

    q_scale, k_scale, v_scale = factors(qe_ref), factors(ke_ref), factors(ve_ref)
    for kv in range(n_kv):
        key, value = head(k_ref, k_scale, kv), head(v_ref, v_scale, kv)
        for y in range(n_y):
            at = slice(y * share, (y + 1) * share)
            for pair in range(n_pair):
                query = head(q_ref, q_scale, (kv * n_y + y) * n_pair + pair)
                rows = jnp.concatenate([query, key[at], value[at]], axis=0)
                o_ref[(y * n_kv + kv) * n_pair + pair] = rows.astype(jnp.bfloat16)


def pack(q_rot, k_rot, v_rot, q_exp, k_exp, v_exp, n_y, n_kv, n_pair):
    tok = q_rot.shape[0]
    vmem = pl.BlockSpec(memory_space=pltpu.VMEM)
    by_head = [e.reshape(-1, HD // HBLK) for e in (q_exp, k_exp, v_exp)]
    return pl.pallas_call(
        functools.partial(pack_kernel, n_y=n_y, n_kv=n_kv, n_pair=n_pair),
        out_shape=jax.ShapeDtypeStruct((n_y * n_kv * n_pair, tok + 2 * tok // n_y, HD), jnp.bfloat16),
        in_specs=[vmem] * 6,
        out_specs=vmem,
        compiler_params=pltpu.CompilerParams(vmem_limit_bytes=32 * 2**20),
        name="pack",
    )(q_rot, k_rot, v_rot, *by_head)


def folded(tile):
    return jnp.sum(tile.reshape(tile.shape[0] // 8, 8, tile.shape[1]), axis=0)


def sign_table():
    i = lax.broadcasted_iota(jnp.int32, (HD, HD), 0)
    j = lax.broadcasted_iota(jnp.int32, (HD, HD), 1)
    both = i & j
    odd = (both ^ (both >> 1) ^ (both >> 2) ^ (both >> 3) ^ (both >> 4)) & 1
    return jnp.where(i // HBLK == j // HBLK, 1.0 - 2.0 * odd.astype(jnp.float32), 0.0).astype(jnp.bfloat16)


def partial_kernel(order_ref, place_ref, kv_ref, *refs, span, targets):
    q_refs, o_refs = refs[:targets], refs[targets:2 * targets]
    rank_ref, q_ref, o_ref, scored, peak, total, acc = refs[2 * targets:]
    group = scored.shape[0] // span
    for n, ref in enumerate(q_refs):
        q_ref[n] = ref[...]
    members = kv_ref.shape[0] // 2
    share = kv_ref.shape[1] // (2 * SPANS_GRP)
    per_chunk = share * QBLK // span
    key_spans = 2 * SPANS_GRP
    first_key = place_ref[0] * SPANS_GRP
    rate = math.log2(math.e) / math.sqrt(HD)
    places = [order_ref[first_key + n] for n in range(key_spans)]
    for n in range(key_spans):
        rank = sum((places[m] < places[n]).astype(jnp.int32) for m in range(key_spans) if m != n)
        rank_ref[rank] = n

    def rows_of(n, half):
        at = half * (SPANS_GRP * share) + lax.rem(n, SPANS_GRP) * share
        tile = kv_ref[pl.ds(lax.div(n, SPANS_GRP) * members, members), pl.ds(pl.multiple_of(at, share), share), :]
        return tile.reshape(span, HD)

    def one(item, _):
        target = lax.div(item, SPANS_GRP)
        a = lax.rem(item, SPANS_GRP)
        q_place = order_ref[place_ref[1 + target] * SPANS_GRP + a]
        count = sum((p <= q_place).astype(jnp.int32) for p in places)
        own = functools.reduce(jnp.logical_or, [p == q_place for p in places])

        at = pl.ds(pl.multiple_of(a * span, span), span)
        q = q_ref[target, at, :]
        peak[...] = jnp.full_like(peak, NEG)
        total[...] = jnp.zeros_like(total)
        acc[...] = jnp.zeros_like(acc)

        def step(t, _):
            slots = [rank_ref[jnp.minimum(t * group + i, key_spans - 1)] for i in range(group)]
            for i, n in enumerate(slots):
                scored[pl.ds(i * span, span), :] = lax.dot_general(rows_of(n, 0), q, NT, preferred_element_type=jnp.float32)
            whole = count - t * group - own.astype(jnp.int32)

            def hide(r, _):
                rows = pl.ds(pl.multiple_of(r * share, share), share)
                inside = lax.broadcasted_iota(jnp.int32, (share, span), 0)
                key_at = inside // per_chunk * QBLK + lax.rem(r, members) * per_chunk + inside % per_chunk
                query_at = lax.broadcasted_iota(jnp.int32, (share, span), 1)
                on_edge = own & (lax.div(r, members) == whole)
                limit = jnp.where(on_edge, 0, -2 * span)
                scored[rows, :] = jnp.where(key_at <= query_at + limit, scored[rows, :], NEG)
                return 0

            lax.fori_loop(jnp.minimum(whole, group) * members, group * members, hide, 0)
            old = peak[...]
            top = old
            for i in range(group):
                top = jnp.maximum(top, jnp.max(scored[pl.ds(i * span, span), :], axis=0, keepdims=True))
            shrink = jnp.exp2((old - top) * rate)
            peak[...] = top
            summed = total[...] * shrink
            added = acc[...] * shrink
            for i, n in enumerate(slots):
                weights = jnp.exp2((scored[pl.ds(i * span, span), :] - top) * rate)
                summed = summed + folded(weights)
                added = added + lax.dot_general(rows_of(n, 1), weights.astype(jnp.bfloat16), TN, preferred_element_type=jnp.float32)
            total[...] = summed
            acc[...] = added
            return 0

        lax.fori_loop(0, lax.div(count + group - 1, group), step, 0)
        summed = jnp.sum(total[...], axis=0, keepdims=True)
        some = summed > 0.0
        safe = jnp.where(some, summed, 1.0)
        o_ref[target, 0:HD, at] = (acc[...] * (1.0 / safe)).astype(jnp.bfloat16)
        level = jnp.where(some, peak[...] * rate + jnp.log2(safe), NEG)
        row = lax.broadcasted_iota(jnp.int32, (TAIL, span), 0)
        tail = jnp.zeros((TAIL, span), jnp.float32)
        for n in range(PARTS):
            part = level.astype(jnp.bfloat16).astype(jnp.float32)
            level = level - part
            tail = jnp.where(row == n, part, tail)
        o_ref[target, HD:HD + TAIL, at] = tail.astype(jnp.bfloat16)
        return 0

    lax.fori_loop(0, targets * SPANS_GRP, one, 0)
    for n, ref in enumerate(o_refs):
        ref[...] = o_ref[n]


def attend_part(order, place, queries, kv):
    targets, rows = len(queries), queries[0].shape[0]
    span = rows // SPANS_GRP
    vmem = pl.BlockSpec(memory_space=pltpu.VMEM)
    smem = pl.BlockSpec(memory_space=pltpu.SMEM)
    keys = 2 * rows
    one = jax.ShapeDtypeStruct((HD + TAIL, rows), jnp.bfloat16)
    return pl.pallas_call(
        functools.partial(partial_kernel, span=span, targets=targets),
        out_shape=[one] * targets,
        in_specs=[smem, smem] + [vmem] * (1 + targets),
        out_specs=[vmem] * targets,
        scratch_shapes=[
            pltpu.SMEM((2 * SPANS_GRP,), jnp.int32),
            pltpu.VMEM((targets, rows, HD), jnp.bfloat16),
            pltpu.VMEM((targets, HD + TAIL, rows), jnp.bfloat16),
            pltpu.VMEM((TILES * span, span), jnp.float32),
            pltpu.VMEM((1, span), jnp.float32),
            pltpu.VMEM((8, span), jnp.float32),
            pltpu.VMEM((HD, span), jnp.float32),
        ],
        compiler_params=pltpu.CompilerParams(vmem_limit_bytes=32 * 2**20),
        cost_estimate=pl.CostEstimate(
            flops=4 * targets * rows * keys * HD, bytes_accessed=3 * 2**20, transcendentals=targets * rows * keys
        ),
        name="attend_part",
    )(order, place, kv, *queries)


def merge_kernel(row_ref, *refs):
    parts, o_ref, flat = refs[:-2], refs[-2], refs[-1]
    rows = o_ref.shape[0]
    levels = []
    for ref in parts:
        tail = ref[HD:HD + TAIL, :].astype(jnp.float32)
        levels.append(jnp.sum(tail, axis=0, keepdims=True))
    top = functools.reduce(jnp.maximum, levels)
    shares = [jnp.exp2(level - top) for level in levels]
    whole = 1.0 / (sum(shares) * math.sqrt(HBLK))
    out = sum(ref[0:HD, :].astype(jnp.float32) * (share * whole) for ref, share in zip(parts, shares))
    high = out.astype(jnp.bfloat16)
    low = (out - high.astype(jnp.float32)).astype(jnp.bfloat16)
    signs = sign_table()
    turned = jnp.dot(signs, high, preferred_element_type=jnp.float32)
    turned = turned + jnp.dot(signs, low, preferred_element_type=jnp.float32)
    flat[...] = turned.astype(jnp.bfloat16)
    block = math.gcd(rows, 256)
    for start in range(0, rows, block):
        want = lax.broadcasted_iota(jnp.int32, (block, rows), 0) + start
        pick = jnp.where(row_ref[...] == want, 1.0, 0.0).astype(jnp.bfloat16)
        o_ref[pl.ds(start, block), :] = lax.dot_general(
            pick, flat[...], NT, preferred_element_type=jnp.float32
        ).astype(jnp.bfloat16)


def merge(row, parts):
    rows = row.shape[1]
    vmem = pl.BlockSpec(memory_space=pltpu.VMEM)
    return pl.pallas_call(
        merge_kernel,
        out_shape=jax.ShapeDtypeStruct((rows, HD), jnp.bfloat16),
        in_specs=[vmem] * (1 + len(parts)),
        out_specs=vmem,
        scratch_shapes=[pltpu.VMEM((HD, rows), jnp.bfloat16)],
        compiler_params=pltpu.CompilerParams(vmem_limit_bytes=32 * 2**20),
        cost_estimate=pl.CostEstimate(flops=2 * rows * rows * HD, bytes_accessed=2 * 2**20, transcendentals=0),
        name="merge",
    )(row, *parts)


def per_device(q_rot, k_rot, v_rot, q_exp, k_exp, v_exp, span_order, ffn_row):
    sizes = {name: lax.axis_size(name) for name in ("x", "core", "y", "kv", "pair")}
    n_x, n_core, n_y, n_kv, n_pair = sizes.values()
    x_at, core_at = lax.axis_index("x"), lax.axis_index("core")
    tok = q_rot.shape[0]
    share = tok // n_y
    plane = n_y * n_kv * n_pair
    message = pack(q_rot, k_rot, v_rot, q_exp, k_exp, v_exp, n_y, n_kv, n_pair)
    got = lax.all_to_all(message, PLANE, split_axis=0, concat_axis=0, tiled=True)
    q_own = got[:, :tok].reshape(plane * tok, HD)
    piece = jnp.concatenate(
        [got[:, tok:tok + share].reshape(plane * share, HD), got[:, tok + share:].reshape(plane * share, HD)], axis=0
    )

    def along_x(array, shift):
        return lax.ppermute(array, "x", [(i, (i + shift) % n_x) for i in range(n_x)])

    shifts = [n_x // 2] + [s for s in range(1, n_x) if s != n_x // 2]
    queries = [along_x(q_own, s) for s in shifts]
    near = n_core * n_y
    kv = lax.all_to_all(
        jnp.broadcast_to(piece[None], (near,) + piece.shape), NEAR, split_axis=0, concat_axis=0, tiled=True
    )

    def place(moves):
        groups = [lax.rem(x_at + n_x - s, n_x) * n_core + core_at for s in moves]
        return jnp.stack([x_at * n_core] + groups).astype(jnp.int32)

    others = attend_part(span_order, place(shifts), queries, kv)
    results = [along_x(part, n_x - s) for part, s in zip(others, shifts)]
    results += attend_part(span_order, place([0]), [q_own], kv)
    placed = merge(ffn_row, results)
    back = lax.all_to_all(placed.reshape(plane, tok, HD), PLANE, split_axis=0, concat_axis=0, tiled=True)
    heads = back.reshape(n_y, n_kv, n_pair, tok, HD).transpose(3, 1, 0, 2, 4)
    return heads.reshape(tok, plane * HD)


def solution(mesh):
    devices = mesh.devices.reshape(4, 2, 4, 8, 2)
    axes = ("x", "core", "y", "kv", "pair")
    inner = Mesh(devices, axes)
    rows = P(axes, None)
    return jax.shard_map(
        per_device,
        mesh=inner,
        in_specs=(rows, rows, rows, rows, rows, rows, P(), P(("x", "core"), None)),
        out_specs=rows,
        check_vma=False,
    )
```

profile of v0, /device:TPU:6, one launch (start us, length us, event | category | flops | bytes accessed | tf_op | source)
XLA Modules:
  0.0 133.9 jit_solution(7886030039151572864)
XLA Ops:
  0.0 0.0 copy-start.5
  0.0 0.0 copy-start.1
  0.0 0.5 broadcast.14
  0.5 0.2 copy-done.5
  0.7 0.7 reduce.9
  1.3 0.0 copy-start.6
  1.4 0.1 reshape.28.qe_ref
  1.5 0.5 copy-done.6
  2.0 0.7 reduce.10
  2.7 0.0 copy-start.7
  2.7 0.1 reshape.29.ke_ref
  2.8 0.6 copy-done.7
  3.3 0.7 reduce.11
  4.0 0.1 reshape.30.ve_ref
  4.1 0.0 copy-done.1
  4.1 0.0 copy-start
  4.1 1.0 copy-done
  5.0 0.0 copy-start.2
  5.0 0.8 copy-done.2
  5.8 0.2 pack.1
  6.0 44.9 %all_to_all.15 = bf16[64,24,128]{2,1,0:T(8,128)(2,1)S(1)} all-to-all(bf16[64,24,128]{2,1,0:T(8,128)(2,1)S(1)} %pack.1), channel_id=1, replica_groups=mesh['x'=4,'core'=2,'y'=4,'kv'=8,'pair'=2] {'y','kv','pair'}, dimensions={0} | all-to-all | bytes 786432 | tf_op jit(solution)/shard_map/all_to_all | solution.py:246
  50.9 1.1 broadcast_in_dim.2
  52.0 4.3 %all-to-all-start.1 = ((bf16[8,512,128]{2,1,0:T(8,128)(2,1)}), bf16[8,512,128]{2,1,0:T(8,128)(2,1)S(1)}, u32[]{:S(2)}, u32[]{:S(2)}) async-start(bf16[8,512,128]{2,1,0:T(8,128)(2,1)} %broadcast_in_dim.2), calls=%async_computation.1 | async-start | bytes 2097152 | tf_op jit(solution)/shard_map/all_to_all | solution.py:258
  56.4 3.3 %collective-permute-start = (bf16[1024,128]{1,0:T(8,128)(2,1)S(1)}, bf16[1024,128]{1,0:T(8,128)(2,1)S(1)}, u32[]{:S(2)}, u32[]{:S(2)}) collective-permute-start(bf16[1024,128]{1,0:T(8,128)(2,1)S(1)} %bitcast.14), channel_id=1, source_target_pairs={{0,256},{128,384},{256,0},{384,128},{1,257},{129,385},{257,1},{385... | collective-permute-start | bytes 786440 | tf_op jit(solution)/shard_map/ppermute | solution.py:253
  59.7 4.0 %collective-permute-start.1 = (bf16[1024,128]{1,0:T(8,128)(2,1)S(1)}, bf16[1024,128]{1,0:T(8,128)(2,1)S(1)}, u32[]{:S(2)}, u32[]{:S(2)}) collective-permute-start(bf16[1024,128]{1,0:T(8,128)(2,1)S(1)} %bitcast.15), channel_id=1, source_target_pairs={{0,128},{128,256},{256,384},{384,0},{1,129},{129,257},{257,385},{3... | collective-permute-start | bytes 786440 | tf_op jit(solution)/shard_map/ppermute | solution.py:253
  63.7 1.9 %collective-permute-start.2 = (bf16[1024,128]{1,0:T(8,128)(2,1)S(1)}, bf16[1024,128]{1,0:T(8,128)(2,1)S(1)}, u32[]{:S(2)}, u32[]{:S(2)}) collective-permute-start(bf16[1024,128]{1,0:T(8,128)(2,1)S(1)} %bitcast.16), channel_id=1, source_target_pairs={{0,384},{128,0},{256,128},{384,256},{1,385},{129,1},{257,129},{385... | collective-permute-start | bytes 786440 | tf_op jit(solution)/shard_map/ppermute | solution.py:253
  65.6 0.0 copy-start.4
  65.7 0.1 pad_add_fusion.place_ref
  65.7 3.0 %collective-permute-done.refs_0_ = bf16[1024,128]{1,0:T(8,128)(2,1)S(1)} collective-permute-done((bf16[1024,128]{1,0:T(8,128)(2,1)S(1)}, bf16[1024,128]{1,0:T(8,128)(2,1)S(1)}, u32[]{:S(2)}, u32[]{:S(2)}) %collective-permute-start) | collective-permute-done | bytes 262176 | tf_op jit(solution)/shard_map/ppermute | solution.py:253
  68.7 3.2 %collective-permute-done.1.refs_1_ = bf16[1024,128]{1,0:T(8,128)(2,1)S(1)} collective-permute-done((bf16[1024,128]{1,0:T(8,128)(2,1)S(1)}, bf16[1024,128]{1,0:T(8,128)(2,1)S(1)}, u32[]{:S(2)}, u32[]{:S(2)}) %collective-permute-start.1) | collective-permute-done | bytes 262176 | tf_op jit(solution)/shard_map/ppermute | solution.py:253
  71.9 3.1 %collective-permute-done.2.refs_2_ = bf16[1024,128]{1,0:T(8,128)(2,1)S(1)} collective-permute-done((bf16[1024,128]{1,0:T(8,128)(2,1)S(1)}, bf16[1024,128]{1,0:T(8,128)(2,1)S(1)}, u32[]{:S(2)}, u32[]{:S(2)}) %collective-permute-start.2) | collective-permute-done | bytes 262176 | tf_op jit(solution)/shard_map/ppermute | solution.py:253
  75.0 0.0 all-to-all-done.1.kv_ref
  75.0 0.0 copy-done.4
  75.0 8.9 %attend_part.2 = (bf16[144,1024]{1,0:T(8,128)(2,1)S(1)}, bf16[144,1024]{1,0:T(8,128)(2,1)S(1)}, bf16[144,1024]{1,0:T(8,128)(2,1)S(1)}) custom-call(s32[16]{0:T(128)S(1)} %copy-done.4, s32[4]{0:T(128)S(1)} %pad_add_fusion.place_ref, bf16[8,512,128]{2,1,0:T(8,128)(2,1)S(1)} %all-to-all-done.1.kv_ref, bf16[1024,128]{1,0:T(8,128)(2,1)S(1)} %collective-permute-done.refs_0_, ...), custom_call_target="tpu_custom_call" | custom-call | flops 3221225472 | bytes 3145728 | tf_op jit(solution)/shard_map/attend_part/pallas_call | solution.py:175
  83.9 1.9 %collective-permute-start.3 = (bf16[144,1024]{1,0:T(8,128)(2,1)S(1)}, bf16[144,1024]{1,0:T(8,128)(2,1)S(1)}, u32[]{:S(2)}, u32[]{:S(2)}) collective-permute-start(bf16[144,1024]{1,0:T(8,128)(2,1)S(1)} %get-tuple-element.8), channel_id=1, source_target_pairs={{0,256},{128,384},{256,0},{384,128},{1,257},{129,385},{257,1},{385... | collective-permute-start | bytes 884744 | tf_op jit(solution)/shard_map/ppermute | solution.py:253
  85.8 5.3 %collective-permute-start.4 = (bf16[144,1024]{1,0:T(8,128)(2,1)S(1)}, bf16[144,1024]{1,0:T(8,128)(2,1)S(1)}, u32[]{:S(2)}, u32[]{:S(2)}) collective-permute-start(bf16[144,1024]{1,0:T(8,128)(2,1)S(1)} %get-tuple-element.9), channel_id=1, source_target_pairs={{0,384},{128,0},{256,128},{384,256},{1,385},{129,1},{257,129},{385... | collective-permute-start | bytes 884744 | tf_op jit(solution)/shard_map/ppermute | solution.py:253
  91.1 4.6 %collective-permute-start.5 = (bf16[144,1024]{1,0:T(8,128)(2,1)S(1)}, bf16[144,1024]{1,0:T(8,128)(2,1)S(1)}, u32[]{:S(2)}, u32[]{:S(2)}) collective-permute-start(bf16[144,1024]{1,0:T(8,128)(2,1)S(1)} %get-tuple-element.10), channel_id=1, source_target_pairs={{0,128},{128,256},{256,384},{384,0},{1,129},{129,257},{257,385},{3... | collective-permute-start | bytes 884744 | tf_op jit(solution)/shard_map/ppermute | solution.py:253
  95.7 0.1 pad_add_fusion.1.place_ref
  95.8 0.0 copy-start.3
  95.8 5.5 %attend_part.3.refs_3_ = bf16[144,1024]{1,0:T(8,128)(2,1)S(1)} custom-call(s32[16]{0:T(128)S(1)} %copy-done.4, s32[2]{0:T(128)S(1)} %pad_add_fusion.1.place_ref, bf16[8,512,128]{2,1,0:T(8,128)(2,1)S(1)} %all-to-all-done.1.kv_ref, bf16[1024,128]{1,0:T(8,128)(2,1)S(1)} %bitcast.17), custom_call_target="tpu_custom_call" | custom-call | flops 1073741824 | bytes 3145728 | tf_op jit(solution)/shard_map/attend_part/pallas_call | solution.py:175
  101.3 0.0 collective-permute-done.3.refs_0_
  101.3 0.7 collective-permute-done.4.refs_1_
  102.1 1.2 collective-permute-done.5.refs_2_
  103.3 0.0 copy-done.3
  103.3 1.2 merge.1
  104.5 28.3 %all_to_all.16 = bf16[64,16,128]{2,1,0:T(8,128)(2,1)S(1)} all-to-all(bf16[64,16,128]{2,1,0:T(8,128)(2,1)S(1)} %bitcast.13), channel_id=1, replica_groups=mesh['x'=4,'core'=2,'y'=4,'kv'=8,'pair'=2] {'y','kv','pair'}, dimensions={0} | all-to-all | bytes 524288 | tf_op jit(solution)/shard_map/all_to_all | solution.py:270
  132.8 0.2 copy.12
  133.0 0.9 reshape.36
  (3 shorter events, 0.1 us)
Async XLA Ops:
  0.0 0.7 copy-start.5
  0.0 4.1 %copy-start.1 = (bf16[16,1024]{1,0:T(8,128)(2,1)S(1)}, bf16[16,1024]{1,0:T(8,128)(2,1)}, u32[]{:S(2)}) copy-start(bf16[16,1024]{1,0:T(8,128)(2,1)} %k_ref.1) | copy-start | bytes 98308
  1.3 0.7 copy-start.6
  2.7 0.7 copy-start.7
  4.1 1.0 copy-start
  5.0 0.8 copy-start.2
  52.0 22.9 %all-to-all-start.1 = ((bf16[8,512,128]{2,1,0:T(8,128)(2,1)}), bf16[8,512,128]{2,1,0:T(8,128)(2,1)S(1)}, u32[]{:S(2)}, u32[]{:S(2)}) async-start(bf16[8,512,128]{2,1,0:T(8,128)(2,1)} %broadcast_in_dim.2), calls=%async_computation.1 | async-start | bytes 2097152 | tf_op jit(solution)/shard_map/all_to_all | solution.py:258
  56.4 12.4 %collective-permute-start = (bf16[1024,128]{1,0:T(8,128)(2,1)S(1)}, bf16[1024,128]{1,0:T(8,128)(2,1)S(1)}, u32[]{:S(2)}, u32[]{:S(2)}) collective-permute-start(bf16[1024,128]{1,0:T(8,128)(2,1)S(1)} %bitcast.14), channel_id=1, source_target_pairs={{0,256},{128,384},{256,0},{384,128},{1,257},{129,385},{257,1},{385... | collective-permute-start | bytes 786440 | tf_op jit(solution)/shard_map/ppermute | solution.py:253
  59.7 12.2 %collective-permute-start.1 = (bf16[1024,128]{1,0:T(8,128)(2,1)S(1)}, bf16[1024,128]{1,0:T(8,128)(2,1)S(1)}, u32[]{:S(2)}, u32[]{:S(2)}) collective-permute-start(bf16[1024,128]{1,0:T(8,128)(2,1)S(1)} %bitcast.15), channel_id=1, source_target_pairs={{0,128},{128,256},{256,384},{384,0},{1,129},{129,257},{257,385},{3... | collective-permute-start | bytes 786440 | tf_op jit(solution)/shard_map/ppermute | solution.py:253
  63.7 11.3 %collective-permute-start.2 = (bf16[1024,128]{1,0:T(8,128)(2,1)S(1)}, bf16[1024,128]{1,0:T(8,128)(2,1)S(1)}, u32[]{:S(2)}, u32[]{:S(2)}) collective-permute-start(bf16[1024,128]{1,0:T(8,128)(2,1)S(1)} %bitcast.16), channel_id=1, source_target_pairs={{0,384},{128,0},{256,128},{384,256},{1,385},{129,1},{257,129},{385... | collective-permute-start | bytes 786440 | tf_op jit(solution)/shard_map/ppermute | solution.py:253
  65.6 9.3 %copy-start.4 = (s32[16]{0:T(128)S(1)}, s32[16]{0:T(128)}, u32[]{:S(2)}) copy-start(s32[16]{0:T(128)} %order_ref.3) | copy-start | bytes 196
  83.9 17.4 %collective-permute-start.3 = (bf16[144,1024]{1,0:T(8,128)(2,1)S(1)}, bf16[144,1024]{1,0:T(8,128)(2,1)S(1)}, u32[]{:S(2)}, u32[]{:S(2)}) collective-permute-start(bf16[144,1024]{1,0:T(8,128)(2,1)S(1)} %get-tuple-element.8), channel_id=1, source_target_pairs={{0,256},{128,384},{256,0},{384,128},{1,257},{129,385},{257,1},{385... | collective-permute-start | bytes 884744 | tf_op jit(solution)/shard_map/ppermute | solution.py:253
  85.8 16.2 %collective-permute-start.4 = (bf16[144,1024]{1,0:T(8,128)(2,1)S(1)}, bf16[144,1024]{1,0:T(8,128)(2,1)S(1)}, u32[]{:S(2)}, u32[]{:S(2)}) collective-permute-start(bf16[144,1024]{1,0:T(8,128)(2,1)S(1)} %get-tuple-element.9), channel_id=1, source_target_pairs={{0,384},{128,0},{256,128},{384,256},{1,385},{129,1},{257,129},{385... | collective-permute-start | bytes 884744 | tf_op jit(solution)/shard_map/ppermute | solution.py:253
  91.1 12.1 %collective-permute-start.5 = (bf16[144,1024]{1,0:T(8,128)(2,1)S(1)}, bf16[144,1024]{1,0:T(8,128)(2,1)S(1)}, u32[]{:S(2)}, u32[]{:S(2)}) collective-permute-start(bf16[144,1024]{1,0:T(8,128)(2,1)S(1)} %get-tuple-element.10), channel_id=1, source_target_pairs={{0,128},{128,256},{256,384},{384,0},{1,129},{129,257},{257,385},{3... | collective-permute-start | bytes 884744 | tf_op jit(solution)/shard_map/ppermute | solution.py:253
  95.8 7.5 %copy-start.3 = (s32[1,1024]{1,0:T(1,128)S(1)}, s32[1,1024]{1,0:T(1,128)}, u32[]{:S(2)}) copy-start(s32[1,1024]{1,0:T(1,128)} %row_ref.1) | copy-start | bytes 12292
where the time goes:
time: 136 us; the launch traced here: 134 us
  blocking collectives  73.1 us (54%)
  starting transfers between devices  25.3 us (19%)
  Pallas kernels  15.8 us (12%)
  waiting for transfers between devices  11.2 us (8%)
  local copies, waits for them, and re-layouts  6.07 us (4%)
  other arithmetic  2.15 us (2%)
    all_to_all x1, blocking collectives, per_device(): lax.all_to_all(message, PLANE, split_axis=0, concat_axis=0, tiled=True)  44.9 us
    all_to_all x1, blocking collectives, per_device(): lax.all_to_all(placed.reshape(plane, tok, HD), PLANE, split_axis=0, conca...  28.3 us
    ppermute x6, starting transfers between devices, along_x(): lax.ppermute(array, 'x', [(i, (i + shift) % n_x) for i in range(n_x)])  21 us
    pallas_call x2, Pallas kernels, attend_part(): pl.pallas_call(functools.partial(partial_kernel, span=span, targets=targe...  14.4 us
    ppermute x6, waiting for transfers between devices, along_x(): lax.ppermute(array, 'x', [(i, (i + shift) % n_x) for i in range(n_x)])  11.2 us
    all_to_all x1, starting transfers between devices, per_device(): lax.all_to_all(jnp.broadcast_to(piece[None], (near,) + piece.shape), NEAR...  4.32 us
    unnamed x17, local copies, waits for them, and re-layouts  3.51 us
  transfers between devices with their start and end apart: 7, of which 5 were waited for; matrix products, arithmetic and copies ran while one was open for 0% of the time, Pallas kernels for 4%

commit v1 on v0

--- a/solution.py
+++ b/solution.py
@@ -23,19 +23,30 @@
 NEAR = ("core", "y")
 
 
-def pack_kernel(q_ref, k_ref, v_ref, qe_ref, ke_ref, ve_ref, o_ref, *, n_y, n_kv, n_pair):
-    tok = q_ref.shape[0]
-    share = tok // n_y
+def factors(ref):
+    width = ref.shape[1]
     blocks = HD // HBLK
-    spread = jnp.where(
-        lax.broadcasted_iota(jnp.int32, (blocks, HD), 1) // HBLK == lax.broadcasted_iota(jnp.int32, (blocks, HD), 0),
-        1.0,
-        0.0,
-    )
-
-    def factors(ref):
-        scale = jnp.exp2(ref[...].astype(jnp.float32))
-        return sum(scale[:, b:b + 1] * spread[b:b + 1, :] for b in range(blocks))
+    heads = width // blocks
+    scale = jnp.exp2(ref[...].astype(jnp.float32))
+    head = lax.broadcasted_iota(jnp.int32, (heads, width), 0)
+    at = lax.broadcasted_iota(jnp.int32, (heads, width), 1)
+    picked = jnp.where(at // blocks == head, scale, 0.0).astype(jnp.bfloat16)
+    at = lax.broadcasted_iota(jnp.int32, (width, HD), 0)
+    lane = lax.broadcasted_iota(jnp.int32, (width, HD), 1)
+    spread = jnp.where(at % blocks == lane // HBLK, 1.0, 0.0).astype(jnp.bfloat16)
+    return jnp.dot(picked, spread, preferred_element_type=jnp.float32)
+
+
+def pack_kernel(*refs, n_y, n_kv, n_pair):
+    count = 6
+    sources, o_ref, held, sems = refs[:count], refs[count], refs[count + 1:2 * count + 1], refs[2 * count + 1]
+    copies = [pltpu.make_async_copy(src, dst, sems.at[n]) for n, (src, dst) in enumerate(zip(sources, held))]
+    for copy in copies:
+        copy.start()
+    for copy in copies:
+        copy.wait()
+    q_ref, k_ref, v_ref, qe_ref, ke_ref, ve_ref = held
+    share = q_ref.shape[0] // n_y
 
     def head(ref, scale, n):
         return ref[:, n * HD:(n + 1) * HD].astype(jnp.float32) * scale[n:n + 1, :]
@@ -51,18 +62,17 @@
                 o_ref[(y * n_kv + kv) * n_pair + pair] = rows.astype(jnp.bfloat16)
 
 
-def pack(q_rot, k_rot, v_rot, q_exp, k_exp, v_exp, n_y, n_kv, n_pair):
-    tok = q_rot.shape[0]
-    vmem = pl.BlockSpec(memory_space=pltpu.VMEM)
-    by_head = [e.reshape(-1, HD // HBLK) for e in (q_exp, k_exp, v_exp)]
+def pack(arrays, n_y, n_kv, n_pair):
+    tok = arrays[0].shape[0]
     return pl.pallas_call(
         functools.partial(pack_kernel, n_y=n_y, n_kv=n_kv, n_pair=n_pair),
         out_shape=jax.ShapeDtypeStruct((n_y * n_kv * n_pair, tok + 2 * tok // n_y, HD), jnp.bfloat16),
-        in_specs=[vmem] * 6,
-        out_specs=vmem,
-        compiler_params=pltpu.CompilerParams(vmem_limit_bytes=32 * 2**20),
+        in_specs=[pl.BlockSpec(memory_space=pl.ANY)] * len(arrays),
+        out_specs=pl.BlockSpec(memory_space=pltpu.VMEM),
+        scratch_shapes=[pltpu.VMEM(a.shape, a.dtype) for a in arrays] + [pltpu.SemaphoreType.DMA((len(arrays),))],
+        compiler_params=pltpu.CompilerParams(vmem_limit_bytes=60 * 2**20),
         name="pack",
-    )(q_rot, k_rot, v_rot, *by_head)
+    )(*arrays)
 
 
 def folded(tile):
@@ -242,12 +252,10 @@
     tok = q_rot.shape[0]
     share = tok // n_y
     plane = n_y * n_kv * n_pair
-    message = pack(q_rot, k_rot, v_rot, q_exp, k_exp, v_exp, n_y, n_kv, n_pair)
+    message = pack((q_rot, k_rot, v_rot, q_exp, k_exp, v_exp), n_y, n_kv, n_pair)
     got = lax.all_to_all(message, PLANE, split_axis=0, concat_axis=0, tiled=True)
     q_own = got[:, :tok].reshape(plane * tok, HD)
-    piece = jnp.concatenate(
-        [got[:, tok:tok + share].reshape(plane * share, HD), got[:, tok + share:].reshape(plane * share, HD)], axis=0
-    )
+    piece = got[:, tok:].reshape(plane, 2, share, HD).transpose(1, 0, 2, 3).reshape(2 * plane * share, HD)
 
     def along_x(array, shift):
         return lax.ppermute(array, "x", [(i, (i + shift) % n_x) for i in range(n_x)])
@@ -263,8 +271,11 @@
         groups = [lax.rem(x_at + n_x - s, n_x) * n_core + core_at for s in moves]
         return jnp.stack([x_at * n_core] + groups).astype(jnp.int32)
 
-    others = attend_part(span_order, place(shifts), queries, kv)
-    results = [along_x(part, n_x - s) for part, s in zip(others, shifts)]
+    far, near_by = shifts[:1], shifts[1:]
+    first = attend_part(span_order, place(far), queries[:1], kv)
+    results = [along_x(part, n_x - s) for part, s in zip(first, far)]
+    others = attend_part(span_order, place(near_by), queries[1:], kv)
+    results += [along_x(part, n_x - s) for part, s in zip(others, near_by)]
     results += attend_part(span_order, place([0]), [q_own], kv)
     placed = merge(ffn_row, results)
     back = lax.all_to_all(placed.reshape(plane, tok, HD), PLANE, split_axis=0, concat_axis=0, tiled=True)

time: 136 us -> 125 us (0.919)
  the two profiles are of different devices: /device:TPU:6 before, /device:TPU:8 now
where the time goes in v1:
time: 125 us
  blocking collectives  68.5 us (55%)
  starting transfers between devices  32.5 us (26%)
  Pallas kernels  15.5 us (12%)
  waiting for transfers between devices  5.36 us (4%)
  local copies, waits for them, and re-layouts  2.33 us (2%)
    all_to_all x1, blocking collectives, per_device(): lax.all_to_all(message, PLANE, split_axis=0, concat_axis=0, tiled=True)  45 us
    ppermute x6, starting transfers between devices, along_x(): lax.ppermute(array, 'x', [(i, (i + shift) % n_x) for i in range(n_x)])  27.6 us
    all_to_all x1, blocking collectives, per_device(): lax.all_to_all(placed.reshape(plane, tok, HD), PLANE, split_axis=0, conca...  23.6 us
    pallas_call x3, Pallas kernels, attend_part(): pl.pallas_call(functools.partial(partial_kernel, span=span, targets=targe...  12.4 us
    all_to_all x1, starting transfers between devices, per_device(): lax.all_to_all(jnp.broadcast_to(piece[None], (near,) + piece.shape), NEAR...  4.91 us
    ppermute x6, waiting for transfers between devices, along_x(): lax.ppermute(array, 'x', [(i, (i + shift) % n_x) for i in range(n_x)])  3.9 us
  transfers between devices with their start and end apart: 7, of which 3 were waited for; matrix products, arithmetic and copies ran while one was open for 0% of the time, Pallas kernels for 10%

profile of v1, /device:TPU:8, one launch (start us, length us, event | category | flops | bytes accessed | tf_op | source)
XLA Modules:
  0.0 124.7 jit_solution(14682084323257770668)
XLA Ops:
  0.0 2.0 %pack.1 = bf16[64,24,128]{2,1,0:T(8,128)(2,1)} custom-call(bf16[16,8192]{1,0:T(8,128)(2,1)} %refs_0_.1, bf16[16,1024]{1,0:T(8,128)(2,1)} %refs_1_.1, bf16[16,1024]{1,0:T(8,128)(2,1)} %refs_2_.1, s32[1,256]{1,0:T(1,128)} %refs_3_.1, s32[1,32]{1,0:T(1,128)} %refs_4_.1, s32[1,32]{1,0:T(1,128)} %refs_5_.1), custom_call_target="tpu_custom_call" | custom-call | tf_op jit(solution)/shard_map/pack/pallas_call | solution.py:67
  2.0 45.0 %all_to_all.15 = bf16[64,24,128]{2,1,0:T(8,128)(2,1)S(1)} all-to-all(bf16[64,24,128]{2,1,0:T(8,128)(2,1)} %pack.1), channel_id=1, replica_groups=mesh['x'=4,'core'=2,'y'=4,'kv'=8,'pair'=2] {'y','kv','pair'}, dimensions={0} | all-to-all | bytes 786432 | tf_op jit(solution)/shard_map/all_to_all | solution.py:256
  47.0 1.1 broadcast_in_dim.8
  48.1 4.9 %all-to-all-start.1 = ((bf16[8,512,128]{2,1,0:T(8,128)(2,1)}), bf16[8,512,128]{2,1,0:T(8,128)(2,1)S(1)}, u32[]{:S(2)}, u32[]{:S(2)}) async-start(bf16[8,512,128]{2,1,0:T(8,128)(2,1)} %broadcast_in_dim.8), calls=%async_computation.1 | async-start | bytes 2097152 | tf_op jit(solution)/shard_map/all_to_all | solution.py:266
  53.0 4.9 %collective-permute-start = (bf16[1024,128]{1,0:T(8,128)(2,1)S(1)}, bf16[1024,128]{1,0:T(8,128)(2,1)S(1)}, u32[]{:S(2)}, u32[]{:S(2)}) collective-permute-start(bf16[1024,128]{1,0:T(8,128)(2,1)S(1)} %bitcast.16), channel_id=1, source_target_pairs={{0,256},{128,384},{256,0},{384,128},{1,257},{129,385},{257,1},{385... | collective-permute-start | bytes 786440 | tf_op jit(solution)/shard_map/ppermute | solution.py:261
  58.0 2.5 %collective-permute-start.2 = (bf16[1024,128]{1,0:T(8,128)(2,1)S(1)}, bf16[1024,128]{1,0:T(8,128)(2,1)S(1)}, u32[]{:S(2)}, u32[]{:S(2)}) collective-permute-start(bf16[1024,128]{1,0:T(8,128)(2,1)S(1)} %bitcast.17), channel_id=1, source_target_pairs={{0,128},{128,256},{256,384},{384,0},{1,129},{129,257},{257,385},{3... | collective-permute-start | bytes 786440 | tf_op jit(solution)/shard_map/ppermute | solution.py:261
  60.5 4.6 %collective-permute-start.3 = (bf16[1024,128]{1,0:T(8,128)(2,1)S(1)}, bf16[1024,128]{1,0:T(8,128)(2,1)S(1)}, u32[]{:S(2)}, u32[]{:S(2)}) collective-permute-start(bf16[1024,128]{1,0:T(8,128)(2,1)S(1)} %bitcast.18), channel_id=1, source_target_pairs={{0,384},{128,0},{256,128},{384,256},{1,385},{129,1},{257,129},{385... | collective-permute-start | bytes 786440 | tf_op jit(solution)/shard_map/ppermute | solution.py:261
  65.0 0.1 pad_add_fusion.place_ref
  65.1 0.0 copy-start.1
  65.1 0.1 pad_add_fusion.1.place_ref
  65.2 0.4 collective-permute-done.refs_0_
  65.6 1.5 %all-to-all-done.1.kv_ref = bf16[8,512,128]{2,1,0:T(8,128)(2,1)S(1)} async-done(((bf16[8,512,128]{2,1,0:T(8,128)(2,1)}), bf16[8,512,128]{2,1,0:T(8,128)(2,1)S(1)}, u32[]{:S(2)}, u32[]{:S(2)}) %all-to-all-start.1) | async-done | bytes 1048608 | tf_op jit(solution)/shard_map/all_to_all | solution.py:266
  67.0 0.0 copy-done.1
  67.0 4.0 %attend_part.3 = bf16[144,1024]{1,0:T(8,128)(2,1)S(1)} custom-call(s32[16]{0:T(128)S(1)} %copy-done.1, s32[2]{0:T(128)S(1)} %pad_add_fusion.place_ref, bf16[8,512,128]{2,1,0:T(8,128)(2,1)S(1)} %all-to-all-done.1.kv_ref, bf16[1024,128]{1,0:T(8,128)(2,1)S(1)} %collective-permute-done.refs_0_), custom_call_target="tpu_custom_call" | custom-call | flops 1073741824 | bytes 3145728 | tf_op jit(solution)/shard_map/attend_part/pallas_call | solution.py:185
  71.0 4.0 %collective-permute-start.1 = (bf16[144,1024]{1,0:T(8,128)(2,1)S(1)}, bf16[144,1024]{1,0:T(8,128)(2,1)S(1)}, u32[]{:S(2)}, u32[]{:S(2)}) collective-permute-start(bf16[144,1024]{1,0:T(8,128)(2,1)S(1)} %attend_part.3), channel_id=1, source_target_pairs={{0,256},{128,384},{256,0},{384,128},{1,257},{129,385},{257,1},{385... | collective-permute-start | bytes 884744 | tf_op jit(solution)/shard_map/ppermute | solution.py:261
  75.0 0.0 collective-permute-done.2.refs_0_
  75.0 0.0 collective-permute-done.3.refs_1_
  75.0 4.1 %attend_part.4 = (bf16[144,1024]{1,0:T(8,128)(2,1)S(1)}, bf16[144,1024]{1,0:T(8,128)(2,1)S(1)}) custom-call(s32[16]{0:T(128)S(1)} %copy-done.1, s32[3]{0:T(128)S(1)} %pad_add_fusion.1.place_ref, bf16[8,512,128]{2,1,0:T(8,128)(2,1)S(1)} %all-to-all-done.1.kv_ref, bf16[1024,128]{1,0:T(8,128)(2,1)S(1)} %collective-permute-done.2.refs_0_, ...), custom_call_target="tpu_custom_call" | custom-call | flops 2147483648 | bytes 3145728 | tf_op jit(solution)/shard_map/attend_part/pallas_call | solution.py:185
  79.2 9.7 %collective-permute-start.4 = (bf16[144,1024]{1,0:T(8,128)(2,1)S(1)}, bf16[144,1024]{1,0:T(8,128)(2,1)S(1)}, u32[]{:S(2)}, u32[]{:S(2)}) collective-permute-start(bf16[144,1024]{1,0:T(8,128)(2,1)S(1)} %get-tuple-element.7), channel_id=1, source_target_pairs={{0,384},{128,0},{256,128},{384,256},{1,385},{129,1},{257,129},{385... | collective-permute-start | bytes 884744 | tf_op jit(solution)/shard_map/ppermute | solution.py:261
  88.9 1.9 %collective-permute-start.5 = (bf16[144,1024]{1,0:T(8,128)(2,1)S(1)}, bf16[144,1024]{1,0:T(8,128)(2,1)S(1)}, u32[]{:S(2)}, u32[]{:S(2)}) collective-permute-start(bf16[144,1024]{1,0:T(8,128)(2,1)S(1)} %get-tuple-element.8), channel_id=1, source_target_pairs={{0,128},{128,256},{256,384},{384,0},{1,129},{129,257},{257,385},{3... | collective-permute-start | bytes 884744 | tf_op jit(solution)/shard_map/ppermute | solution.py:261
  90.8 0.1 pad_add_fusion.2.place_ref
  90.9 0.0 copy-start
  90.9 4.3 %attend_part.5.refs_3_ = bf16[144,1024]{1,0:T(8,128)(2,1)S(1)} custom-call(s32[16]{0:T(128)S(1)} %copy-done.1, s32[2]{0:T(128)S(1)} %pad_add_fusion.2.place_ref, bf16[8,512,128]{2,1,0:T(8,128)(2,1)S(1)} %all-to-all-done.1.kv_ref, bf16[1024,128]{1,0:T(8,128)(2,1)S(1)} %bitcast.19), custom_call_target="tpu_custom_call" | custom-call | flops 1073741824 | bytes 3145728 | tf_op jit(solution)/shard_map/attend_part/pallas_call | solution.py:185
  95.2 0.0 collective-permute-done.1.refs_0_
  95.2 0.0 collective-permute-done.4.refs_1_
  95.2 3.5 %collective-permute-done.5.refs_2_ = bf16[144,1024]{1,0:T(8,128)(2,1)S(1)} collective-permute-done((bf16[144,1024]{1,0:T(8,128)(2,1)S(1)}, bf16[144,1024]{1,0:T(8,128)(2,1)S(1)}, u32[]{:S(2)}, u32[]{:S(2)}) %collective-permute-start.5) | collective-permute-done | bytes 294944 | tf_op jit(solution)/shard_map/ppermute | solution.py:261
  98.7 0.0 copy-done
  98.7 1.2 merge.1
  99.9 23.6 %all_to_all.16 = bf16[64,16,128]{2,1,0:T(8,128)(2,1)S(1)} all-to-all(bf16[64,16,128]{2,1,0:T(8,128)(2,1)S(1)} %bitcast.15), channel_id=1, replica_groups=mesh['x'=4,'core'=2,'y'=4,'kv'=8,'pair'=2] {'y','kv','pair'}, dimensions={0} | all-to-all | bytes 524288 | tf_op jit(solution)/shard_map/all_to_all | solution.py:281
  123.5 0.2 copy.12
  123.8 0.9 reshape.20
  (3 shorter events, 0.1 us)
Async XLA Ops:
  48.1 18.9 %all-to-all-start.1 = ((bf16[8,512,128]{2,1,0:T(8,128)(2,1)}), bf16[8,512,128]{2,1,0:T(8,128)(2,1)S(1)}, u32[]{:S(2)}, u32[]{:S(2)}) async-start(bf16[8,512,128]{2,1,0:T(8,128)(2,1)} %broadcast_in_dim.8), calls=%async_computation.1 | async-start | bytes 2097152 | tf_op jit(solution)/shard_map/all_to_all | solution.py:266
  53.0 12.5 %collective-permute-start = (bf16[1024,128]{1,0:T(8,128)(2,1)S(1)}, bf16[1024,128]{1,0:T(8,128)(2,1)S(1)}, u32[]{:S(2)}, u32[]{:S(2)}) collective-permute-start(bf16[1024,128]{1,0:T(8,128)(2,1)S(1)} %bitcast.16), channel_id=1, source_target_pairs={{0,256},{128,384},{256,0},{384,128},{1,257},{129,385},{257,1},{385... | collective-permute-start | bytes 786440 | tf_op jit(solution)/shard_map/ppermute | solution.py:261
  58.0 17.0 %collective-permute-start.2 = (bf16[1024,128]{1,0:T(8,128)(2,1)S(1)}, bf16[1024,128]{1,0:T(8,128)(2,1)S(1)}, u32[]{:S(2)}, u32[]{:S(2)}) collective-permute-start(bf16[1024,128]{1,0:T(8,128)(2,1)S(1)} %bitcast.17), channel_id=1, source_target_pairs={{0,128},{128,256},{256,384},{384,0},{1,129},{129,257},{257,385},{3... | collective-permute-start | bytes 786440 | tf_op jit(solution)/shard_map/ppermute | solution.py:261
  60.5 14.5 %collective-permute-start.3 = (bf16[1024,128]{1,0:T(8,128)(2,1)S(1)}, bf16[1024,128]{1,0:T(8,128)(2,1)S(1)}, u32[]{:S(2)}, u32[]{:S(2)}) collective-permute-start(bf16[1024,128]{1,0:T(8,128)(2,1)S(1)} %bitcast.18), channel_id=1, source_target_pairs={{0,384},{128,0},{256,128},{384,256},{1,385},{129,1},{257,129},{385... | collective-permute-start | bytes 786440 | tf_op jit(solution)/shard_map/ppermute | solution.py:261
  65.1 1.9 %copy-start.1 = (s32[16]{0:T(128)S(1)}, s32[16]{0:T(128)}, u32[]{:S(2)}) copy-start(s32[16]{0:T(128)} %order_ref.5) | copy-start | bytes 196
  71.0 24.2 %collective-permute-start.1 = (bf16[144,1024]{1,0:T(8,128)(2,1)S(1)}, bf16[144,1024]{1,0:T(8,128)(2,1)S(1)}, u32[]{:S(2)}, u32[]{:S(2)}) collective-permute-start(bf16[144,1024]{1,0:T(8,128)(2,1)S(1)} %attend_part.3), channel_id=1, source_target_pairs={{0,256},{128,384},{256,0},{384,128},{1,257},{129,385},{257,1},{385... | collective-permute-start | bytes 884744 | tf_op jit(solution)/shard_map/ppermute | solution.py:261
  79.2 16.0 %collective-permute-start.4 = (bf16[144,1024]{1,0:T(8,128)(2,1)S(1)}, bf16[144,1024]{1,0:T(8,128)(2,1)S(1)}, u32[]{:S(2)}, u32[]{:S(2)}) collective-permute-start(bf16[144,1024]{1,0:T(8,128)(2,1)S(1)} %get-tuple-element.7), channel_id=1, source_target_pairs={{0,384},{128,0},{256,128},{384,256},{1,385},{129,1},{257,129},{385... | collective-permute-start | bytes 884744 | tf_op jit(solution)/shard_map/ppermute | solution.py:261
  88.9 9.8 %collective-permute-start.5 = (bf16[144,1024]{1,0:T(8,128)(2,1)S(1)}, bf16[144,1024]{1,0:T(8,128)(2,1)S(1)}, u32[]{:S(2)}, u32[]{:S(2)}) collective-permute-start(bf16[144,1024]{1,0:T(8,128)(2,1)S(1)} %get-tuple-element.8), channel_id=1, source_target_pairs={{0,128},{128,256},{256,384},{384,0},{1,129},{129,257},{257,385},{3... | collective-permute-start | bytes 884744 | tf_op jit(solution)/shard_map/ppermute | solution.py:261
  90.9 7.8 %copy-start = (s32[1,1024]{1,0:T(1,128)S(1)}, s32[1,1024]{1,0:T(1,128)}, u32[]{:S(2)}) copy-start(s32[1,1024]{1,0:T(1,128)} %row_ref.1) | copy-start | bytes 12292

commit v2 on v1

v2 whole, which is shorter than its diff:
```python
import functools
import math

import jax
import jax.numpy as jnp
from jax import lax
from jax.experimental import pallas as pl
from jax.experimental.pallas import tpu as pltpu
from jax.sharding import Mesh, PartitionSpec as P

HD = 128
HBLK = 32
QBLK = 16
SPANS_GRP = 2
PARTS = 3
TAIL = 16
LOW, HIGH = 2.0**-80, 2.0**110

NEG = -1e30
NT = (((1,), (1,)), ((), ()))
TN = (((0,), (0,)), ((), ()))
PLANE = ("y", "kv", "pair")
ROW = ("xh", "xl")
NEAR = ("xl", "y")


def factors(ref):
    width = ref.shape[1]
    blocks = HD // HBLK
    heads = width // blocks
    scale = jnp.exp2(ref[...].astype(jnp.float32))
    head = lax.broadcasted_iota(jnp.int32, (heads, width), 0)
    at = lax.broadcasted_iota(jnp.int32, (heads, width), 1)
    picked = jnp.where(at // blocks == head, scale, 0.0).astype(jnp.bfloat16)
    at = lax.broadcasted_iota(jnp.int32, (width, HD), 0)
    lane = lax.broadcasted_iota(jnp.int32, (width, HD), 1)
    spread = jnp.where(at % blocks == lane // HBLK, 1.0, 0.0).astype(jnp.bfloat16)
    return jnp.dot(picked, spread, preferred_element_type=jnp.float32)


def pack_kernel(*refs, n_y, n_kv, n_pair):
    count = 6
    sources, o_ref, held, sems = refs[:count], refs[count], refs[count + 1:2 * count + 1], refs[2 * count + 1]
    copies = [pltpu.make_async_copy(src, dst, sems.at[n]) for n, (src, dst) in enumerate(zip(sources, held))]
    for copy in copies:
        copy.start()
    for copy in copies:
        copy.wait()
    q_ref, k_ref, v_ref, qe_ref, ke_ref, ve_ref = held
    share = q_ref.shape[0] // n_y

    def head(ref, scale, n):
        return ref[:, n * HD:(n + 1) * HD].astype(jnp.float32) * scale[n:n + 1, :]

    q_scale, k_scale, v_scale = factors(qe_ref), factors(ke_ref), factors(ve_ref)
    for kv in range(n_kv):
        key, value = head(k_ref, k_scale, kv), head(v_ref, v_scale, kv)
        for y in range(n_y):
            at = slice(y * share, (y + 1) * share)
            for pair in range(n_pair):
                query = head(q_ref, q_scale, (kv * n_y + y) * n_pair + pair)
                rows = jnp.concatenate([query, key[at], value[at]], axis=0)
                o_ref[(y * n_kv + kv) * n_pair + pair] = rows.astype(jnp.bfloat16)


def pack(arrays, n_y, n_kv, n_pair):
    tok = arrays[0].shape[0]
    return pl.pallas_call(
        functools.partial(pack_kernel, n_y=n_y, n_kv=n_kv, n_pair=n_pair),
        out_shape=jax.ShapeDtypeStruct((n_y * n_kv * n_pair, tok + 2 * tok // n_y, HD), jnp.bfloat16),
        in_specs=[pl.BlockSpec(memory_space=pl.ANY)] * len(arrays),
        out_specs=pl.BlockSpec(memory_space=pltpu.VMEM),
        scratch_shapes=[pltpu.VMEM(a.shape, a.dtype) for a in arrays] + [pltpu.SemaphoreType.DMA((len(arrays),))],
        compiler_params=pltpu.CompilerParams(vmem_limit_bytes=60 * 2**20),
        name="pack",
    )(*arrays)


def folded(tile):
    return jnp.sum(tile.reshape(tile.shape[0] // 8, 8, tile.shape[1]), axis=0)


def sign_table():
    i = lax.broadcasted_iota(jnp.int32, (HD, HD), 0)
    j = lax.broadcasted_iota(jnp.int32, (HD, HD), 1)
    both = i & j
    odd = (both ^ (both >> 1) ^ (both >> 2) ^ (both >> 3) ^ (both >> 4)) & 1
    return jnp.where(i // HBLK == j // HBLK, 1.0 - 2.0 * odd.astype(jnp.float32), 0.0).astype(jnp.bfloat16)


def partial_kernel(order_ref, place_ref, *refs, span, targets, groups, edge):
    kv_refs, q_refs, o_refs = refs[:2], refs[2:2 + targets], refs[2 + targets:2 + 2 * targets]
    q_ref, o_ref, key, value, least, most, scored, peak, total, acc = refs[2 + 2 * targets:]
    members = 2 * kv_refs[0].shape[0] // groups
    share = kv_refs[0].shape[1] // (2 * SPANS_GRP)
    per_chunk = share * QBLK // span
    key_spans = groups * SPANS_GRP
    rate = math.log2(math.e) / math.sqrt(HD)
    places = [order_ref[place_ref[n // SPANS_GRP] * SPANS_GRP + n % SPANS_GRP] for n in range(key_spans)]

    for n, ref in enumerate(q_refs):
        q_ref[n] = ref[...]
    for n in range(key_spans):
        rank = sum((places[m] < places[n]).astype(jnp.int32) for m in range(key_spans) if m != n)
        at = pl.ds(pl.multiple_of(rank * span, span), span)
        for half, ref in enumerate((key, value)):
            kv_ref, group = kv_refs[n // (key_spans // 2)], n // SPANS_GRP % (groups // 2)
            start = (half * SPANS_GRP + n % SPANS_GRP) * share
            rows = kv_ref[pl.ds(group * members, members), pl.ds(start, share), :]
            ref[at, :] = rows.reshape(span, HD)
    least[...] = jnp.ones_like(least)
    most[...] = jnp.ones_like(most)

    def shown(s, q_index):
        inside = lax.broadcasted_iota(jnp.int32, s.shape, 0)
        chunk = inside % share
        key_at = chunk // per_chunk * QBLK + inside // share * per_chunk + chunk % per_chunk
        return key_at <= lax.broadcasted_iota(jnp.int32, s.shape, 1) + q_index

    def write(target, at, summed, level):
        o_ref[target, 0:HD, at] = (acc[...] * (1.0 / summed)).astype(jnp.bfloat16)
        row = lax.broadcasted_iota(jnp.int32, (TAIL, span), 0)
        tail = jnp.zeros((TAIL, span), jnp.float32)
        for n in range(PARTS):
            part = level.astype(jnp.bfloat16).astype(jnp.float32)
            level = level - part
            tail = jnp.where(row == n, part, tail)
        o_ref[target, HD:HD + TAIL, at] = tail.astype(jnp.bfloat16)

    def sight(item):
        target = lax.div(item, SPANS_GRP)
        a = lax.rem(item, SPANS_GRP)
        q_place = order_ref[place_ref[groups + target] * SPANS_GRP + a]
        count = sum((p <= q_place).astype(jnp.int32) for p in places)
        own = functools.reduce(jnp.logical_or, [p == q_place for p in places])
        at = pl.ds(pl.multiple_of(a * span, span), span)
        return target, at, count, count - own.astype(jnp.int32)

    def one(item, _):
        target, at, count, whole = sight(item)
        q = q_ref[target, at, :]
        total[...] = jnp.zeros_like(total)
        acc[...] = jnp.zeros_like(acc)

        def add(start, width, masked):
            rows = pl.ds(pl.multiple_of(start * span, span), width * span)
            s = lax.dot_general(key[rows, :], q, NT, preferred_element_type=jnp.float32) * rate
            if masked:
                s = jnp.where(shown(s, jnp.where(start < whole, span, 0)), s, NEG)
            weights = jnp.exp2(s)
            total[...] += folded(weights)
            acc[...] += lax.dot_general(
                value[rows, :], weights.astype(jnp.bfloat16), TN, preferred_element_type=jnp.float32
            )

        def two(t, _):
            add(2 * t, 2, False)
            return 0

        def single(t, _):
            add(t, 1, edge)
            return 0

        pairs = lax.div(whole, 2)
        lax.fori_loop(0, pairs, two, 0)
        lax.fori_loop(2 * pairs, count, single, 0)
        summed = jnp.sum(total[...], axis=0, keepdims=True)
        summed = jnp.where(count > 0, summed, 1.0)
        least[...] = jnp.minimum(least[...], summed)
        most[...] = jnp.maximum(most[...], summed)
        write(target, at, summed, jnp.where(count > 0, jnp.log2(summed), NEG))
        return 0

    lax.fori_loop(0, targets * SPANS_GRP, one, 0)

    def again(item, _):
        target, at, count, whole = sight(item)
        q = q_ref[target, at, :]
        peak[...] = jnp.full_like(peak, NEG)
        total[...] = jnp.zeros_like(total)
        acc[...] = jnp.zeros_like(acc)

        def step(t, _):
            rows = pl.ds(pl.multiple_of(t * span, span), span)
            s = lax.dot_general(key[rows, :], q, NT, preferred_element_type=jnp.float32)
            scored[...] = jnp.where(shown(s, jnp.where(t < whole, span, 0)), s, NEG)
            old = peak[...]
            top = jnp.maximum(old, jnp.max(scored[...], axis=0, keepdims=True))
            shrink = jnp.exp2((old - top) * rate)
            weights = jnp.exp2((scored[...] - top) * rate)
            peak[...] = top
            total[...] = total[...] * shrink + folded(weights)
            acc[...] = acc[...] * shrink + lax.dot_general(
                value[rows, :], weights.astype(jnp.bfloat16), TN, preferred_element_type=jnp.float32
            )
            return 0

        lax.fori_loop(0, count, step, 0)
        summed = jnp.sum(total[...], axis=0, keepdims=True)
        summed = jnp.where(count > 0, summed, 1.0)
        write(target, at, summed, jnp.where(count > 0, peak[...] * rate + jnp.log2(summed), NEG))
        return 0

    safe = (jnp.min(least[...]) > LOW) & (jnp.max(most[...]) < HIGH)

    @pl.when(jnp.logical_not(safe))
    def _():
        lax.fori_loop(0, targets * SPANS_GRP, again, 0)

    for n, ref in enumerate(o_refs):
        ref[...] = o_ref[n]


def attend_part(order, place, queries, kv, edge):
    targets, rows = len(queries), queries[0].shape[0]
    span = rows // SPANS_GRP
    vmem = pl.BlockSpec(memory_space=pltpu.VMEM)
    smem = pl.BlockSpec(memory_space=pltpu.SMEM)
    groups = sum(part.shape[0] * part.shape[1] for part in kv) // (2 * rows)
    keys = groups * rows
    one = jax.ShapeDtypeStruct((HD + TAIL, rows), jnp.bfloat16)
    return pl.pallas_call(
        functools.partial(partial_kernel, span=span, targets=targets, groups=groups, edge=edge),
        out_shape=[one] * targets,
        in_specs=[smem, smem] + [vmem] * (2 + targets),
        out_specs=[vmem] * targets,
        scratch_shapes=[
            pltpu.VMEM((targets, rows, HD), jnp.bfloat16),
            pltpu.VMEM((targets, HD + TAIL, rows), jnp.bfloat16),
            pltpu.VMEM((keys, HD), jnp.bfloat16),
            pltpu.VMEM((keys, HD), jnp.bfloat16),
            pltpu.VMEM((1, span), jnp.float32),
            pltpu.VMEM((1, span), jnp.float32),
            pltpu.VMEM((span, span), jnp.float32),
            pltpu.VMEM((1, span), jnp.float32),
            pltpu.VMEM((8, span), jnp.float32),
            pltpu.VMEM((HD, span), jnp.float32),
        ],
        compiler_params=pltpu.CompilerParams(vmem_limit_bytes=32 * 2**20),
        cost_estimate=pl.CostEstimate(
            flops=4 * targets * rows * keys * HD, bytes_accessed=3 * 2**20, transcendentals=targets * rows * keys
        ),
        name="attend_part",
    )(order, place, *kv, *queries)


def merge_kernel(row_ref, *refs):
    parts, o_ref, flat = refs[:-2], refs[-2], refs[-1]
    rows = o_ref.shape[0]
    levels = []
    for ref in parts:
        tail = ref[HD:HD + TAIL, :].astype(jnp.float32)
        levels.append(jnp.sum(tail, axis=0, keepdims=True))
    top = functools.reduce(jnp.maximum, levels)
    shares = [jnp.exp2(level - top) for level in levels]
    whole = 1.0 / (sum(shares) * math.sqrt(HBLK))
    out = sum(ref[0:HD, :].astype(jnp.float32) * (share * whole) for ref, share in zip(parts, shares))
    high = out.astype(jnp.bfloat16)
    low = (out - high.astype(jnp.float32)).astype(jnp.bfloat16)
    signs = sign_table()
    turned = jnp.dot(signs, high, preferred_element_type=jnp.float32)
    turned = turned + jnp.dot(signs, low, preferred_element_type=jnp.float32)
    flat[...] = turned.astype(jnp.bfloat16)
    block = math.gcd(rows, 256)
    for start in range(0, rows, block):
        want = lax.broadcasted_iota(jnp.int32, (block, rows), 0) + start
        pick = jnp.where(row_ref[...] == want, 1.0, 0.0).astype(jnp.bfloat16)
        o_ref[pl.ds(start, block), :] = lax.dot_general(
            pick, flat[...], NT, preferred_element_type=jnp.float32
        ).astype(jnp.bfloat16)


def merge(row, parts):
    rows = row.shape[1]
    vmem = pl.BlockSpec(memory_space=pltpu.VMEM)
    return pl.pallas_call(
        merge_kernel,
        out_shape=jax.ShapeDtypeStruct((rows, HD), jnp.bfloat16),
        in_specs=[vmem] * (1 + len(parts)),
        out_specs=vmem,
        scratch_shapes=[pltpu.VMEM((HD, rows), jnp.bfloat16)],
        compiler_params=pltpu.CompilerParams(vmem_limit_bytes=32 * 2**20),
        cost_estimate=pl.CostEstimate(flops=2 * rows * rows * HD, bytes_accessed=2 * 2**20, transcendentals=0),
        name="merge",
    )(row, *parts)


def per_device(q_rot, k_rot, v_rot, q_exp, k_exp, v_exp, span_order, ffn_row):
    n_xl, n_y, n_kv, n_pair = (lax.axis_size(name) for name in ("xl", "y", "kv", "pair"))
    n_x, n_core = lax.axis_size(ROW), lax.axis_size("core")
    x_at, core_at = lax.axis_index(ROW), lax.axis_index("core")
    tok = q_rot.shape[0]
    share = tok // n_y
    plane = n_y * n_kv * n_pair
    message = pack((q_rot, k_rot, v_rot, q_exp, k_exp, v_exp), n_y, n_kv, n_pair)
    got = lax.all_to_all(message, PLANE, split_axis=0, concat_axis=0, tiled=True)
    q_own = got[:, :tok].reshape(plane * tok, HD)
    piece = got[:, tok:].reshape(plane, 2, share, HD).transpose(1, 0, 2, 3).reshape(2 * plane * share, HD)

    def across(array):
        return lax.ppermute(array, ROW, [(i, n_x - 1 - i) for i in range(n_x)])

    q_far = across(q_own)
    near = n_xl * n_y
    kv = lax.all_to_all(
        jnp.broadcast_to(piece[None], (near,) + piece.shape), NEAR, split_axis=0, concat_axis=0, tiled=True
    )
    kv, q_far = lax.optimization_barrier((kv, q_far))
    kv = (kv, lax.ppermute(kv, "core", [(0, 1), (1, 0)]))
    first = lax.div(x_at, n_xl) * n_xl
    held = [(first + i) * n_core + c for c in (core_at, 1 - core_at) for i in range(n_xl)]

    def place(x):
        return jnp.stack(held + [x * n_core + core_at]).astype(jnp.int32)

    far, = attend_part(span_order, place(n_x - 1 - x_at), [q_far], kv, False)
    own, = attend_part(span_order, place(x_at), [q_own], kv, True)
    results = [across(far), own]
    placed = merge(ffn_row, results)
    back = lax.all_to_all(placed.reshape(plane, tok, HD), PLANE, split_axis=0, concat_axis=0, tiled=True)
    heads = back.reshape(n_y, n_kv, n_pair, tok, HD).transpose(3, 1, 0, 2, 4)
    return heads.reshape(tok, plane * HD)


def solution(mesh):
    devices = mesh.devices.reshape(2, 2, 2, 4, 8, 2)
    axes = ("xh", "xl", "core", "y", "kv", "pair")
    inner = Mesh(devices, axes)
    rows = P(axes, None)
    return jax.shard_map(
        per_device,
        mesh=inner,
        in_specs=(rows, rows, rows, rows, rows, rows, P(), P(("xh", "xl", "core"), None)),
        out_specs=rows,
        check_vma=False,
    )
```

time: 125 us -> 133 us (1.064)
  the two profiles are of different devices: /device:TPU:8 before, /device:TPU:1 now
where the time goes in v2:
time: 133 us; the launch traced here: 132 us
  blocking collectives  67.1 us (50%)
  starting transfers between devices  32.6 us (25%)
  Pallas kernels  21.9 us (16%)
  waiting for transfers between devices  7.94 us (6%)
  local copies, waits for them, and re-layouts  2.5 us (2%)
    all_to_all x1, blocking collectives, per_device(): lax.all_to_all(message, PLANE, split_axis=0, concat_axis=0, tiled=True)  44 us
    all_to_all x1, blocking collectives, per_device(): lax.all_to_all(placed.reshape(plane, tok, HD), PLANE, split_axis=0, conca...  23.1 us
    ppermute x2, starting transfers between devices, across(): return lax.ppermute(array, ROW, [(i, n_x - 1 - i) for i in range(n_x)])  20.9 us
    pallas_call x2, Pallas kernels, attend_part(): pl.pallas_call(functools.partial(partial_kernel, span=span, targets=targe...  18.9 us
    ppermute x1, starting transfers between devices, per_device(): kv = (kv, lax.ppermute(kv, 'core', [(0, 1), (1, 0)]))  7.19 us
    all_to_all x1, starting transfers between devices, per_device(): lax.all_to_all(jnp.broadcast_to(piece[None], (near,) + piece.shape), NEAR...  4.49 us
    ppermute x2, waiting for transfers between devices, across(): return lax.ppermute(array, ROW, [(i, n_x - 1 - i) for i in range(n_x)])  3.89 us
  transfers between devices with their start and end apart: 4, of which 3 were waited for; matrix products, arithmetic and copies ran while one was open for 0% of the time, Pallas kernels for 12%

profile of v2, /device:TPU:1, one launch (start us, length us, event | category | flops | bytes accessed | tf_op | source)
XLA Modules:
  0.0 132.3 jit_solution(7184403005028279399)
XLA Ops:
  0.0 2.0 %pack.1 = bf16[64,24,128]{2,1,0:T(8,128)(2,1)} custom-call(bf16[16,8192]{1,0:T(8,128)(2,1)} %refs_0_.1, bf16[16,1024]{1,0:T(8,128)(2,1)} %refs_1_.1, bf16[16,1024]{1,0:T(8,128)(2,1)} %refs_2_.1, s32[1,256]{1,0:T(1,128)} %refs_3_.1, s32[1,32]{1,0:T(1,128)} %refs_4_.1, s32[1,32]{1,0:T(1,128)} %refs_5_.1), custom_call_target="tpu_custom_call" | custom-call | tf_op jit(solution)/shard_map/pack/pallas_call | solution.py:68
  2.0 44.0 %all_to_all.15 = bf16[64,24,128]{2,1,0:T(8,128)(2,1)S(1)} all-to-all(bf16[64,24,128]{2,1,0:T(8,128)(2,1)} %pack.1), channel_id=1, replica_groups=mesh['xh'=2,'xl'=2,'core'=2,'y'=4,'kv'=8,'pair'=2] {'y','kv','pair'}, dimensions={0} | all-to-all | bytes 786432 | tf_op jit(solution)/shard_map/all_to_all | solution.py:296
  46.1 1.1 broadcast_in_dim.8
  47.2 4.5 %all-to-all-start.1 = ((bf16[8,512,128]{2,1,0:T(8,128)(2,1)}), bf16[8,512,128]{2,1,0:T(8,128)(2,1)S(1)}, u32[]{:S(2)}, u32[]{:S(2)}) async-start(bf16[8,512,128]{2,1,0:T(8,128)(2,1)} %broadcast_in_dim.8), calls=%async_computation.1 | async-start | bytes 2097152 | tf_op jit(solution)/shard_map/all_to_all | solution.py:305
  51.7 4.6 %collective-permute-start = (bf16[1024,128]{1,0:T(8,128)(2,1)S(1)}, bf16[1024,128]{1,0:T(8,128)(2,1)S(1)}, u32[]{:S(2)}, u32[]{:S(2)}) collective-permute-start(bf16[1024,128]{1,0:T(8,128)(2,1)S(1)} %bitcast.16), channel_id=1, source_target_pairs={{0,384},{128,256},{256,128},{384,0},{1,385},{129,257},{257,129},{3... | collective-permute-start | bytes 786440 | tf_op jit(solution)/shard_map/ppermute | solution.py:301
  56.3 3.9 %collective-permute-done.refs_2_ = bf16[1024,128]{1,0:T(8,128)(2,1)S(1)} collective-permute-done((bf16[1024,128]{1,0:T(8,128)(2,1)S(1)}, bf16[1024,128]{1,0:T(8,128)(2,1)S(1)}, u32[]{:S(2)}, u32[]{:S(2)}) %collective-permute-start) | collective-permute-done | bytes 262176 | tf_op jit(solution)/shard_map/ppermute | solution.py:301
  60.2 1.9 %all-to-all-done.1.refs_0_ = bf16[8,512,128]{2,1,0:T(8,128)(2,1)S(1)} async-done(((bf16[8,512,128]{2,1,0:T(8,128)(2,1)}), bf16[8,512,128]{2,1,0:T(8,128)(2,1)S(1)}, u32[]{:S(2)}, u32[]{:S(2)}) %all-to-all-start.1) | async-done | bytes 1048608 | tf_op jit(solution)/shard_map/all_to_all | solution.py:305
  62.1 7.2 %collective-permute-start.1 = (bf16[8,512,128]{2,1,0:T(8,128)(2,1)S(1)}, bf16[8,512,128]{2,1,0:T(8,128)(2,1)S(1)}, u32[]{:S(2)}, u32[]{:S(2)}) collective-permute-start(bf16[8,512,128]{2,1,0:T(8,128)(2,1)S(1)} %all-to-all-done.1.refs_0_), channel_id=1, source_target_pairs={{0,64},{64,0},{1,65},{65,1},{2,66},{66,2},{3,67},{67,3},{4,68},{68... | collective-permute-start | bytes 3145736 | tf_op jit(solution)/shard_map/ppermute | solution.py:309
  69.3 0.0 copy-start.1
  69.4 0.1 stack.33.place_ref
  69.4 2.1 %collective-permute-done.1.refs_1_ = bf16[8,512,128]{2,1,0:T(8,128)(2,1)S(1)} collective-permute-done((bf16[8,512,128]{2,1,0:T(8,128)(2,1)S(1)}, bf16[8,512,128]{2,1,0:T(8,128)(2,1)S(1)}, u32[]{:S(2)}, u32[]{:S(2)}) %collective-permute-start.1) | collective-permute-done | bytes 1048608 | tf_op jit(solution)/shard_map/ppermute | solution.py:309
  71.6 0.0 copy-done.1
  71.6 3.6 %attend_part.2 = bf16[144,1024]{1,0:T(8,128)(2,1)S(1)} custom-call(s32[16]{0:T(128)S(1)} %copy-done.1, s32[5]{0:T(128)S(1)} %stack.33.place_ref, bf16[8,512,128]{2,1,0:T(8,128)(2,1)S(1)} %all-to-all-done.1.refs_0_, bf16[8,512,128]{2,1,0:T(8,128)(2,1)S(1)} %collective-permute-done.1.refs_1_, bf16[1024,128]{1,0:T(8,128)(2,1)S(1)} %collective-permute-done.refs_2_), custom_call_target="tpu_custom_call" | custom-call | flops 2147483648 | bytes 3145728 | tf_op jit(solution)/shard_map/attend_part/pallas_call | solution.py:222
  75.2 16.3 %collective-permute-start.2 = (bf16[144,1024]{1,0:T(8,128)(2,1)S(1)}, bf16[144,1024]{1,0:T(8,128)(2,1)S(1)}, u32[]{:S(2)}, u32[]{:S(2)}) collective-permute-start(bf16[144,1024]{1,0:T(8,128)(2,1)S(1)} %attend_part.2), channel_id=1, source_target_pairs={{0,384},{128,256},{256,128},{384,0},{1,385},{129,257},{257,129},{3... | collective-permute-start | bytes 884744 | tf_op jit(solution)/shard_map/ppermute | solution.py:301
  91.5 0.1 stack.35.place_ref
  91.5 0.0 copy-start
  91.5 15.3 %attend_part.3.refs_1_ = bf16[144,1024]{1,0:T(8,128)(2,1)S(1)} custom-call(s32[16]{0:T(128)S(1)} %copy-done.1, s32[5]{0:T(128)S(1)} %stack.35.place_ref, bf16[8,512,128]{2,1,0:T(8,128)(2,1)S(1)} %all-to-all-done.1.refs_0_, bf16[8,512,128]{2,1,0:T(8,128)(2,1)S(1)} %collective-permute-done.1.refs_1_, bf16[1024,128]{1,0:T(8,128)(2,1)S(1)} %bitcast.17), custom_call_target="tpu_custom_call" | custom-call | flops 2147483648 | bytes 3145728 | tf_op jit(solution)/shard_map/attend_part/pallas_call | solution.py:222
  106.9 0.0 collective-permute-done.2.refs_0_
  106.9 0.0 copy-done
  106.9 1.1 merge.1
  108.0 23.1 %all_to_all.16 = bf16[64,16,128]{2,1,0:T(8,128)(2,1)S(1)} all-to-all(bf16[64,16,128]{2,1,0:T(8,128)(2,1)S(1)} %bitcast.18), channel_id=1, replica_groups=mesh['xh'=2,'xl'=2,'core'=2,'y'=4,'kv'=8,'pair'=2] {'y','kv','pair'}, dimensions={0} | all-to-all | bytes 524288 | tf_op jit(solution)/shard_map/all_to_all | solution.py:320
  131.1 0.2 copy.12
  131.4 0.9 reshape.20
  (3 shorter events, 0.1 us)
Async XLA Ops:
  47.2 14.9 %all-to-all-start.1 = ((bf16[8,512,128]{2,1,0:T(8,128)(2,1)}), bf16[8,512,128]{2,1,0:T(8,128)(2,1)S(1)}, u32[]{:S(2)}, u32[]{:S(2)}) async-start(bf16[8,512,128]{2,1,0:T(8,128)(2,1)} %broadcast_in_dim.8), calls=%async_computation.1 | async-start | bytes 2097152 | tf_op jit(solution)/shard_map/all_to_all | solution.py:305
  51.7 8.5 %collective-permute-start = (bf16[1024,128]{1,0:T(8,128)(2,1)S(1)}, bf16[1024,128]{1,0:T(8,128)(2,1)S(1)}, u32[]{:S(2)}, u32[]{:S(2)}) collective-permute-start(bf16[1024,128]{1,0:T(8,128)(2,1)S(1)} %bitcast.16), channel_id=1, source_target_pairs={{0,384},{128,256},{256,128},{384,0},{1,385},{129,257},{257,129},{3... | collective-permute-start | bytes 786440 | tf_op jit(solution)/shard_map/ppermute | solution.py:301
  62.1 9.5 %collective-permute-start.1 = (bf16[8,512,128]{2,1,0:T(8,128)(2,1)S(1)}, bf16[8,512,128]{2,1,0:T(8,128)(2,1)S(1)}, u32[]{:S(2)}, u32[]{:S(2)}) collective-permute-start(bf16[8,512,128]{2,1,0:T(8,128)(2,1)S(1)} %all-to-all-done.1.refs_0_), channel_id=1, source_target_pairs={{0,64},{64,0},{1,65},{65,1},{2,66},{66,2},{3,67},{67,3},{4,68},{68... | collective-permute-start | bytes 3145736 | tf_op jit(solution)/shard_map/ppermute | solution.py:309
  69.3 2.2 %copy-start.1 = (s32[16]{0:T(128)S(1)}, s32[16]{0:T(128)}, u32[]{:S(2)}) copy-start(s32[16]{0:T(128)} %order_ref.3) | copy-start | bytes 196
  75.2 31.7 %collective-permute-start.2 = (bf16[144,1024]{1,0:T(8,128)(2,1)S(1)}, bf16[144,1024]{1,0:T(8,128)(2,1)S(1)}, u32[]{:S(2)}, u32[]{:S(2)}) collective-permute-start(bf16[144,1024]{1,0:T(8,128)(2,1)S(1)} %attend_part.2), channel_id=1, source_target_pairs={{0,384},{128,256},{256,128},{384,0},{1,385},{129,257},{257,129},{3... | collective-permute-start | bytes 884744 | tf_op jit(solution)/shard_map/ppermute | solution.py:301
  91.5 15.3 %copy-start = (s32[1,1024]{1,0:T(1,128)S(1)}, s32[1,1024]{1,0:T(1,128)}, u32[]{:S(2)}) copy-start(s32[1,1024]{1,0:T(1,128)} %row_ref.1) | copy-start | bytes 12292

commit v3 on v2

--- a/solution.py
+++ b/solution.py
@@ -14,6 +14,7 @@
 SPANS_GRP = 2
 PARTS = 3
 TAIL = 16
+ONES = 8
 LOW, HIGH = 2.0**-80, 2.0**110
 
 NEG = -1e30
@@ -88,9 +89,8 @@
     return jnp.where(i // HBLK == j // HBLK, 1.0 - 2.0 * odd.astype(jnp.float32), 0.0).astype(jnp.bfloat16)
 
 
-def partial_kernel(order_ref, place_ref, *refs, span, targets, groups, edge):
-    kv_refs, q_refs, o_refs = refs[:2], refs[2:2 + targets], refs[2 + targets:2 + 2 * targets]
-    q_ref, o_ref, key, value, least, most, scored, peak, total, acc = refs[2 + 2 * targets:]
+def partial_kernel(order_ref, place_ref, near_ref, other_ref, q_ref, o_ref, key, value, least, most, scored, peak, acc, *, span, groups, edge):
+    kv_refs = (near_ref, other_ref)
     members = 2 * kv_refs[0].shape[0] // groups
     share = kv_refs[0].shape[1] // (2 * SPANS_GRP)
     per_chunk = share * QBLK // span
@@ -98,8 +98,6 @@
     rate = math.log2(math.e) / math.sqrt(HD)
     places = [order_ref[place_ref[n // SPANS_GRP] * SPANS_GRP + n % SPANS_GRP] for n in range(key_spans)]
 
-    for n, ref in enumerate(q_refs):
-        q_ref[n] = ref[...]
     for n in range(key_spans):
         rank = sum((places[m] < places[n]).astype(jnp.int32) for m in range(key_spans) if m != n)
         at = pl.ds(pl.multiple_of(rank * span, span), span)
@@ -107,7 +105,8 @@
             kv_ref, group = kv_refs[n // (key_spans // 2)], n // SPANS_GRP % (groups // 2)
             start = (half * SPANS_GRP + n % SPANS_GRP) * share
             rows = kv_ref[pl.ds(group * members, members), pl.ds(start, share), :]
-            ref[at, :] = rows.reshape(span, HD)
+            ref[at, 0:HD] = rows.reshape(span, HD)
+    value[:, HD:HD + ONES] = jnp.ones((value.shape[0], ONES), value.dtype)
     least[...] = jnp.ones_like(least)
     most[...] = jnp.ones_like(most)
 
@@ -117,29 +116,26 @@
         key_at = chunk // per_chunk * QBLK + inside // share * per_chunk + chunk % per_chunk
         return key_at <= lax.broadcasted_iota(jnp.int32, s.shape, 1) + q_index
 
-    def write(target, at, summed, level):
-        o_ref[target, 0:HD, at] = (acc[...] * (1.0 / summed)).astype(jnp.bfloat16)
+    def write(at, summed, level):
+        o_ref[0:HD, at] = (acc[0:HD, :] * (1.0 / summed)).astype(o_ref.dtype)
         row = lax.broadcasted_iota(jnp.int32, (TAIL, span), 0)
         tail = jnp.zeros((TAIL, span), jnp.float32)
         for n in range(PARTS):
             part = level.astype(jnp.bfloat16).astype(jnp.float32)
             level = level - part
             tail = jnp.where(row == n, part, tail)
-        o_ref[target, HD:HD + TAIL, at] = tail.astype(jnp.bfloat16)
-
-    def sight(item):
-        target = lax.div(item, SPANS_GRP)
-        a = lax.rem(item, SPANS_GRP)
-        q_place = order_ref[place_ref[groups + target] * SPANS_GRP + a]
+        o_ref[HD:HD + TAIL, at] = tail.astype(o_ref.dtype)
+
+    def sight(a):
+        q_place = order_ref[place_ref[groups] * SPANS_GRP + a]
         count = sum((p <= q_place).astype(jnp.int32) for p in places)
         own = functools.reduce(jnp.logical_or, [p == q_place for p in places])
         at = pl.ds(pl.multiple_of(a * span, span), span)
-        return target, at, count, count - own.astype(jnp.int32)
-
-    def one(item, _):
-        target, at, count, whole = sight(item)
-        q = q_ref[target, at, :]
-        total[...] = jnp.zeros_like(total)
+        return at, count, count - own.astype(jnp.int32)
+
+    def one(a, _):
+        at, count, whole = sight(a)
+        q = q_ref[at, :]
         acc[...] = jnp.zeros_like(acc)
 
         def add(start, width, masked):
@@ -147,11 +143,8 @@
             s = lax.dot_general(key[rows, :], q, NT, preferred_element_type=jnp.float32) * rate
             if masked:
                 s = jnp.where(shown(s, jnp.where(start < whole, span, 0)), s, NEG)
-            weights = jnp.exp2(s)
-            total[...] += folded(weights)
-            acc[...] += lax.dot_general(
-                value[rows, :], weights.astype(jnp.bfloat16), TN, preferred_element_type=jnp.float32
-            )
+            weights = jnp.exp2(s).astype(jnp.bfloat16)
+            acc[...] += lax.dot_general(value[rows, :], weights, TN, preferred_element_type=jnp.float32)
 
         def two(t, _):
             add(2 * t, 2, False)
@@ -164,20 +157,19 @@
         pairs = lax.div(whole, 2)
         lax.fori_loop(0, pairs, two, 0)
         lax.fori_loop(2 * pairs, count, single, 0)
-        summed = jnp.sum(total[...], axis=0, keepdims=True)
+        summed = acc[HD:HD + 1, :]
         summed = jnp.where(count > 0, summed, 1.0)
         least[...] = jnp.minimum(least[...], summed)
         most[...] = jnp.maximum(most[...], summed)
-        write(target, at, summed, jnp.where(count > 0, jnp.log2(summed), NEG))
+        write(at, summed, jnp.where(count > 0, jnp.log2(summed), NEG))
         return 0
 
-    lax.fori_loop(0, targets * SPANS_GRP, one, 0)
-
-    def again(item, _):
-        target, at, count, whole = sight(item)
-        q = q_ref[target, at, :]
+    lax.fori_loop(0, SPANS_GRP, one, 0)
+
+    def again(a, _):
+        at, count, whole = sight(a)
+        q = q_ref[at, :]
         peak[...] = jnp.full_like(peak, NEG)
-        total[...] = jnp.zeros_like(total)
         acc[...] = jnp.zeros_like(acc)
 
         def step(t, _):
@@ -189,59 +181,51 @@
             shrink = jnp.exp2((old - top) * rate)
             weights = jnp.exp2((scored[...] - top) * rate)
             peak[...] = top
-            total[...] = total[...] * shrink + folded(weights)
             acc[...] = acc[...] * shrink + lax.dot_general(
                 value[rows, :], weights.astype(jnp.bfloat16), TN, preferred_element_type=jnp.float32
             )
             return 0
 
         lax.fori_loop(0, count, step, 0)
-        summed = jnp.sum(total[...], axis=0, keepdims=True)
+        summed = acc[HD:HD + 1, :]
         summed = jnp.where(count > 0, summed, 1.0)
-        write(target, at, summed, jnp.where(count > 0, peak[...] * rate + jnp.log2(summed), NEG))
+        write(at, summed, jnp.where(count > 0, peak[...] * rate + jnp.log2(summed), NEG))
         return 0
 
     safe = (jnp.min(least[...]) > LOW) & (jnp.max(most[...]) < HIGH)
 
     @pl.when(jnp.logical_not(safe))
     def _():
-        lax.fori_loop(0, targets * SPANS_GRP, again, 0)
-
-    for n, ref in enumerate(o_refs):
-        ref[...] = o_ref[n]
-
-
-def attend_part(order, place, queries, kv, edge):
-    targets, rows = len(queries), queries[0].shape[0]
+        lax.fori_loop(0, SPANS_GRP, again, 0)
+
+
+def attend_part(order, place, query, kv, edge, dtype):
+    rows = query.shape[0]
     span = rows // SPANS_GRP
     vmem = pl.BlockSpec(memory_space=pltpu.VMEM)
     smem = pl.BlockSpec(memory_space=pltpu.SMEM)
     groups = sum(part.shape[0] * part.shape[1] for part in kv) // (2 * rows)
     keys = groups * rows
-    one = jax.ShapeDtypeStruct((HD + TAIL, rows), jnp.bfloat16)
     return pl.pallas_call(
-        functools.partial(partial_kernel, span=span, targets=targets, groups=groups, edge=edge),
-        out_shape=[one] * targets,
-        in_specs=[smem, smem] + [vmem] * (2 + targets),
-        out_specs=[vmem] * targets,
+        functools.partial(partial_kernel, span=span, groups=groups, edge=edge),
+        out_shape=jax.ShapeDtypeStruct((HD + TAIL, rows), dtype),
+        in_specs=[smem, smem] + [vmem] * 3,
+        out_specs=vmem,
         scratch_shapes=[
-            pltpu.VMEM((targets, rows, HD), jnp.bfloat16),
-            pltpu.VMEM((targets, HD + TAIL, rows), jnp.bfloat16),
             pltpu.VMEM((keys, HD), jnp.bfloat16),
-            pltpu.VMEM((keys, HD), jnp.bfloat16),
+            pltpu.VMEM((keys, HD + ONES), jnp.bfloat16),
             pltpu.VMEM((1, span), jnp.float32),
             pltpu.VMEM((1, span), jnp.float32),
             pltpu.VMEM((span, span), jnp.float32),
             pltpu.VMEM((1, span), jnp.float32),
-            pltpu.VMEM((8, span), jnp.float32),
-            pltpu.VMEM((HD, span), jnp.float32),
+            pltpu.VMEM((HD + ONES, span), jnp.float32),
         ],
         compiler_params=pltpu.CompilerParams(vmem_limit_bytes=32 * 2**20),
         cost_estimate=pl.CostEstimate(
-            flops=4 * targets * rows * keys * HD, bytes_accessed=3 * 2**20, transcendentals=targets * rows * keys
+            flops=4 * rows * keys * HD, bytes_accessed=3 * 2**20, transcendentals=rows * keys
         ),
         name="attend_part",
-    )(order, place, *kv, *queries)
+    )(order, place, *kv, query)
 
 
 def merge_kernel(row_ref, *refs):
@@ -313,8 +297,8 @@
     def place(x):
         return jnp.stack(held + [x * n_core + core_at]).astype(jnp.int32)
 
-    far, = attend_part(span_order, place(n_x - 1 - x_at), [q_far], kv, False)
-    own, = attend_part(span_order, place(x_at), [q_own], kv, True)
+    far = attend_part(span_order, place(n_x - 1 - x_at), q_far, kv, False, jnp.bfloat16)
+    own = attend_part(span_order, place(x_at), q_own, kv, True, jnp.float32)
     results = [across(far), own]
     placed = merge(ffn_row, results)
     back = lax.all_to_all(placed.reshape(plane, tok, HD), PLANE, split_axis=0, concat_axis=0, tiled=True)

time: 133 us -> 132 us (level)
  the two profiles are of different devices: /device:TPU:1 before, /device:TPU:6 now
where the time goes in v3:
time: 132 us
  blocking collectives  68.7 us (52%)
  Pallas kernels  24.3 us (18%)
  starting transfers between devices  23.7 us (18%)
  waiting for transfers between devices  12.4 us (9%)
  local copies, waits for them, and re-layouts  2.5 us (2%)
    all_to_all x1, blocking collectives, per_device(): lax.all_to_all(message, PLANE, split_axis=0, concat_axis=0, tiled=True)  45.1 us
    all_to_all x1, blocking collectives, per_device(): lax.all_to_all(placed.reshape(plane, tok, HD), PLANE, split_axis=0, conca...  23.6 us
    pallas_call x2, Pallas kernels, attend_part(): pl.pallas_call(functools.partial(partial_kernel, span=span, groups=groups...  21.3 us
    ppermute x2, starting transfers between devices, across(): return lax.ppermute(array, ROW, [(i, n_x - 1 - i) for i in range(n_x)])  16 us
    ppermute x2, waiting for transfers between devices, across(): return lax.ppermute(array, ROW, [(i, n_x - 1 - i) for i in range(n_x)])  7.55 us
    all_to_all x1, starting transfers between devices, per_device(): lax.all_to_all(jnp.broadcast_to(piece[None], (near,) + piece.shape), NEAR...  5.78 us
  transfers between devices with their start and end apart: 4, of which 3 were waited for; matrix products, arithmetic and copies ran while one was open for 0% of the time, Pallas kernels for 12%

profile of v3, /device:TPU:6, one launch (start us, length us, event | category | flops | bytes accessed | tf_op | source)
XLA Modules:
  0.0 131.8 jit_solution(16349294837552051880)
XLA Ops:
  0.0 2.0 %pack.1 = bf16[64,24,128]{2,1,0:T(8,128)(2,1)} custom-call(bf16[16,8192]{1,0:T(8,128)(2,1)} %refs_0_.1, bf16[16,1024]{1,0:T(8,128)(2,1)} %refs_1_.1, bf16[16,1024]{1,0:T(8,128)(2,1)} %refs_2_.1, s32[1,256]{1,0:T(1,128)} %refs_3_.1, s32[1,32]{1,0:T(1,128)} %refs_4_.1, s32[1,32]{1,0:T(1,128)} %refs_5_.1), custom_call_target="tpu_custom_call" | custom-call | tf_op jit(solution)/shard_map/pack/pallas_call | solution.py:69
  2.0 45.1 %all_to_all.15 = bf16[64,24,128]{2,1,0:T(8,128)(2,1)S(1)} all-to-all(bf16[64,24,128]{2,1,0:T(8,128)(2,1)} %pack.1), channel_id=1, replica_groups=mesh['xh'=2,'xl'=2,'core'=2,'y'=4,'kv'=8,'pair'=2] {'y','kv','pair'}, dimensions={0} | all-to-all | bytes 786432 | tf_op jit(solution)/shard_map/all_to_all | solution.py:280
  47.1 1.1 broadcast_in_dim.8
  48.2 5.8 %all-to-all-start.1 = ((bf16[8,512,128]{2,1,0:T(8,128)(2,1)}), bf16[8,512,128]{2,1,0:T(8,128)(2,1)S(1)}, u32[]{:S(2)}, u32[]{:S(2)}) async-start(bf16[8,512,128]{2,1,0:T(8,128)(2,1)} %broadcast_in_dim.8), calls=%async_computation.1 | async-start | bytes 2097152 | tf_op jit(solution)/shard_map/all_to_all | solution.py:289
  54.0 1.9 %collective-permute-start = (bf16[1024,128]{1,0:T(8,128)(2,1)S(1)}, bf16[1024,128]{1,0:T(8,128)(2,1)S(1)}, u32[]{:S(2)}, u32[]{:S(2)}) collective-permute-start(bf16[1024,128]{1,0:T(8,128)(2,1)S(1)} %bitcast.17), channel_id=1, source_target_pairs={{0,384},{128,256},{256,128},{384,0},{1,385},{129,257},{257,129},{3... | collective-permute-start | bytes 786440 | tf_op jit(solution)/shard_map/ppermute | solution.py:285
  56.0 7.5 %collective-permute-done.q_ref = bf16[1024,128]{1,0:T(8,128)(2,1)S(1)} collective-permute-done((bf16[1024,128]{1,0:T(8,128)(2,1)S(1)}, bf16[1024,128]{1,0:T(8,128)(2,1)S(1)}, u32[]{:S(2)}, u32[]{:S(2)}) %collective-permute-start) | collective-permute-done | bytes 262176 | tf_op jit(solution)/shard_map/ppermute | solution.py:285
  63.5 2.4 %all-to-all-done.1.near_ref = bf16[8,512,128]{2,1,0:T(8,128)(2,1)S(1)} async-done(((bf16[8,512,128]{2,1,0:T(8,128)(2,1)}), bf16[8,512,128]{2,1,0:T(8,128)(2,1)S(1)}, u32[]{:S(2)}, u32[]{:S(2)}) %all-to-all-start.1) | async-done | bytes 1048608 | tf_op jit(solution)/shard_map/all_to_all | solution.py:289
  65.9 1.9 %collective-permute-start.1 = (bf16[8,512,128]{2,1,0:T(8,128)(2,1)S(1)}, bf16[8,512,128]{2,1,0:T(8,128)(2,1)S(1)}, u32[]{:S(2)}, u32[]{:S(2)}) collective-permute-start(bf16[8,512,128]{2,1,0:T(8,128)(2,1)S(1)} %all-to-all-done.1.near_ref), channel_id=1, source_target_pairs={{0,64},{64,0},{1,65},{65,1},{2,66},{66,2},{3,67},{67,3},{4,68},{68... | collective-permute-start | bytes 3145736 | tf_op jit(solution)/shard_map/ppermute | solution.py:293
  67.8 0.0 copy-start.1
  67.8 0.1 stack.33.place_ref
  67.9 2.5 %collective-permute-done.1.other_ref = bf16[8,512,128]{2,1,0:T(8,128)(2,1)S(1)} collective-permute-done((bf16[8,512,128]{2,1,0:T(8,128)(2,1)S(1)}, bf16[8,512,128]{2,1,0:T(8,128)(2,1)S(1)}, u32[]{:S(2)}, u32[]{:S(2)}) %collective-permute-start.1) | collective-permute-done | bytes 1048608 | tf_op jit(solution)/shard_map/ppermute | solution.py:293
  70.4 0.0 copy-done.1
  70.4 5.3 %attend_part.2 = bf16[144,1024]{1,0:T(8,128)(2,1)S(1)} custom-call(s32[16]{0:T(128)S(1)} %copy-done.1, s32[5]{0:T(128)S(1)} %stack.33.place_ref, bf16[8,512,128]{2,1,0:T(8,128)(2,1)S(1)} %all-to-all-done.1.near_ref, bf16[8,512,128]{2,1,0:T(8,128)(2,1)S(1)} %collective-permute-done.1.other_ref, bf16[1024,128]{1,0:T(8,128)(2,1)S(1)} %collective-permute-done.q_ref), custom_call_target="tpu_custom_call" | custom-call | flops 2147483648 | bytes 3145728 | tf_op jit(solution)/shard_map/attend_part/pallas_call | solution.py:209
  75.7 14.1 %collective-permute-start.2 = (bf16[144,1024]{1,0:T(8,128)(2,1)S(1)}, bf16[144,1024]{1,0:T(8,128)(2,1)S(1)}, u32[]{:S(2)}, u32[]{:S(2)}) collective-permute-start(bf16[144,1024]{1,0:T(8,128)(2,1)S(1)} %attend_part.2), channel_id=1, source_target_pairs={{0,384},{128,256},{256,128},{384,0},{1,385},{129,257},{257,129},{3... | collective-permute-start | bytes 884744 | tf_op jit(solution)/shard_map/ppermute | solution.py:285
  89.8 0.1 stack.35.place_ref
  89.9 0.0 copy-start
  89.9 16.0 %attend_part.3.refs_1_ = f32[144,1024]{1,0:T(8,128)S(1)} custom-call(s32[16]{0:T(128)S(1)} %copy-done.1, s32[5]{0:T(128)S(1)} %stack.35.place_ref, bf16[8,512,128]{2,1,0:T(8,128)(2,1)S(1)} %all-to-all-done.1.near_ref, bf16[8,512,128]{2,1,0:T(8,128)(2,1)S(1)} %collective-permute-done.1.other_ref, bf16[1024,128]{1,0:T(8,128)(2,1)S(1)} %bitcast.18), custom_call_target="tpu_custom_call" | custom-call | flops 2147483648 | bytes 3145728 | tf_op jit(solution)/shard_map/attend_part/pallas_call | solution.py:209
  105.9 0.0 collective-permute-done.2.refs_0_
  105.9 0.0 copy-done
  105.9 1.1 merge.1
  107.0 23.6 %all_to_all.16 = bf16[64,16,128]{2,1,0:T(8,128)(2,1)S(1)} all-to-all(bf16[64,16,128]{2,1,0:T(8,128)(2,1)S(1)} %bitcast.16), channel_id=1, replica_groups=mesh['xh'=2,'xl'=2,'core'=2,'y'=4,'kv'=8,'pair'=2] {'y','kv','pair'}, dimensions={0} | all-to-all | bytes 524288 | tf_op jit(solution)/shard_map/all_to_all | solution.py:304
  130.6 0.2 copy.12
  130.9 0.9 reshape.20
  (3 shorter events, 0.1 us)
Async XLA Ops:
  48.2 17.6 %all-to-all-start.1 = ((bf16[8,512,128]{2,1,0:T(8,128)(2,1)}), bf16[8,512,128]{2,1,0:T(8,128)(2,1)S(1)}, u32[]{:S(2)}, u32[]{:S(2)}) async-start(bf16[8,512,128]{2,1,0:T(8,128)(2,1)} %broadcast_in_dim.8), calls=%async_computation.1 | async-start | bytes 2097152 | tf_op jit(solution)/shard_map/all_to_all | solution.py:289
  54.0 9.5 %collective-permute-start = (bf16[1024,128]{1,0:T(8,128)(2,1)S(1)}, bf16[1024,128]{1,0:T(8,128)(2,1)S(1)}, u32[]{:S(2)}, u32[]{:S(2)}) collective-permute-start(bf16[1024,128]{1,0:T(8,128)(2,1)S(1)} %bitcast.17), channel_id=1, source_target_pairs={{0,384},{128,256},{256,128},{384,0},{1,385},{129,257},{257,129},{3... | collective-permute-start | bytes 786440 | tf_op jit(solution)/shard_map/ppermute | solution.py:285
  65.9 4.5 %collective-permute-start.1 = (bf16[8,512,128]{2,1,0:T(8,128)(2,1)S(1)}, bf16[8,512,128]{2,1,0:T(8,128)(2,1)S(1)}, u32[]{:S(2)}, u32[]{:S(2)}) collective-permute-start(bf16[8,512,128]{2,1,0:T(8,128)(2,1)S(1)} %all-to-all-done.1.near_ref), channel_id=1, source_target_pairs={{0,64},{64,0},{1,65},{65,1},{2,66},{66,2},{3,67},{67,3},{4,68},{68... | collective-permute-start | bytes 3145736 | tf_op jit(solution)/shard_map/ppermute | solution.py:293
  67.8 2.6 %copy-start.1 = (s32[16]{0:T(128)S(1)}, s32[16]{0:T(128)}, u32[]{:S(2)}) copy-start(s32[16]{0:T(128)} %order_ref.3) | copy-start | bytes 196
  75.7 30.2 %collective-permute-start.2 = (bf16[144,1024]{1,0:T(8,128)(2,1)S(1)}, bf16[144,1024]{1,0:T(8,128)(2,1)S(1)}, u32[]{:S(2)}, u32[]{:S(2)}) collective-permute-start(bf16[144,1024]{1,0:T(8,128)(2,1)S(1)} %attend_part.2), channel_id=1, source_target_pairs={{0,384},{128,256},{256,128},{384,0},{1,385},{129,257},{257,129},{3... | collective-permute-start | bytes 884744 | tf_op jit(solution)/shard_map/ppermute | solution.py:285
  89.9 16.0 %copy-start = (s32[1,1024]{1,0:T(1,128)S(1)}, s32[1,1024]{1,0:T(1,128)}, u32[]{:S(2)}) copy-start(s32[1,1024]{1,0:T(1,128)} %row_ref.1) | copy-start | bytes 12292
